TPU v7x, 32 devices: a whole 2x2x4 slice. The times are simulated.
32 devices in a mesh: dp: 8 (over y, x, core), expert: 4 (over z).
Axes of the slice: x: 2, y: 2, z: 4, core: 2. Of those that a mesh axis runs over, the one named last changes fastest.
Arguments:
- tokens: bfloat16 [256, 4096], P(('dp', 'expert')), may hold values from -6 to 6
- expert_ids: int32 [256, 8], P(('dp', 'expert')), may hold values from 0 to 15, all different within a row; in each aligned block of 8 rows (0 to 7, 8 to 15, ...) at most 8 rows name the same one
- router: bfloat16 [16, 4096], replicated, may hold values from -0.09375 to 0.09375
- w_gate: bfloat16 [16, 1536, 4096], P('dp', 'expert'), may hold values from -0.09375 to 0.09375
- w_up: bfloat16 [16, 1536, 4096], P('dp', 'expert'), may hold values from -0.09375 to 0.09375
- w_down: bfloat16 [16, 1536, 4096], P('dp', 'expert'), may hold values from -0.15625 to 0.15625
Outputs:
- mixed: bfloat16 [256, 4096], P(('dp', 'expert'))
Inputs may be any that keep to these rules, and one draw needn't show every extreme that they name: `expert_ids`: each row names 8 different experts. Within the rows of one device (aligned blocks of 8 rows) no expert is named by more than 8 rows, and in some block one expert is named by exactly 8 rows.
All inputs are finite; a program needn't handle non-finite values.
Results may differ from a plain program's by a relative error of at most 0.0049.
Values may be sent and summed in bfloat16 or wider, within the bound.
No kernel may reach another device: no remote copies, remote signals or barrier semaphores. Data moves between devices by JAX's collectives and lax.ppermute only.
A program may use at most 192 MiB of HBM per device.

v0:
```python
import functools

import jax
import jax.numpy as jnp
from jax import lax
from jax.experimental import pallas as pl
from jax.experimental.pallas import tpu as pltpu
from jax.sharding import PartitionSpec as P

LANES = 128
ROWS = 256
COPIES = 4
VMEM_BYTES = 36 * 1024 * 1024
IN_VMEM = pl.BlockSpec(memory_space=pltpu.VMEM)
ANYWHERE = pl.BlockSpec(memory_space=pl.ANY)


def times_rows(left, right):
    return lax.dot_general(
        left, right, (((1,), (1,)), ((), ())), preferred_element_type=jnp.float32
    )


def swap(value, axis, mask):
    count = lax.axis_size(axis)
    return lax.ppermute(value, axis, [(i, i ^ mask) for i in range(count)])


def swap_sum(value, axis, mask):
    return swap(value.astype(jnp.bfloat16), axis, mask).astype(jnp.float32)


def squares():
    plane = [1 << bit for bit in range(1, lax.axis_size("dp").bit_length() - 1)]
    x_masks, y_masks = plane[: len(plane) // 2], plane[len(plane) // 2 :]
    return [(("dp", x), ("dp", y)) for x, y in zip(x_masks, y_masks)]


CORE = ("dp", 1)


def cat(parts):
    return parts[0] if len(parts) == 1 else jnp.concatenate(parts)


def split(value, count):
    step = value.shape[0] // count
    return [value[start : start + step] for start in range(0, value.shape[0], step)]


def gather_rows(block, w_gate, w_up):
    depth = lax.axis_size("expert")
    column = [block] + [swap(block, "expert", mask) for mask in range(1, depth)]
    near, far = cat(column[: depth // 2]), cat(column[depth // 2 :])
    near, held_gate = lax.optimization_barrier((near, hold(w_gate)))
    far, w_up = lax.optimization_barrier((far, w_up))
    held_up = hold(w_up)
    levels = squares()
    for level, (x, y) in enumerate(levels):
        near_x, near_y = swap(near, *x), swap(near, *y)
        far_x, far_y = swap(far, *x), swap(far, *y)
        if level == 0:
            near_x, far_y, held_up = lax.optimization_barrier((near_x, far_y, held_up))
        near_d, far_d = swap(near_x, *y), swap(far_y, *x)
        if level < len(levels) - 1:
            near, far = cat([near, near_x, near_y, near_d]), cat([far, far_x, far_y, far_d])
    groups = [cat([near, far]), cat([near_x, near_y, far_x, far_y]), cat([near_d, far_d])]
    return groups, [swap(group, *CORE) for group in groups], held_gate, held_up


def scatter_sums(kept, away):
    def joined(index):
        return kept[index] + swap(away[index], *CORE).astype(jnp.float32)

    near_d, far_d = split(joined(2), 2)
    near_x, near_y, far_x, far_y = split(joined(1), 4)
    near, far = split(joined(0), 2)
    levels = squares()[::-1]
    for level, (x, y) in enumerate(levels):
        if level > 0:
            near, near_x, near_y, near_d = split(near, 4)
            far, far_x, far_y, far_d = split(far, 4)
        far_y = far_y + swap_sum(far_d, *x)
        near_x = near_x + swap_sum(near_d, *y)
        far = far + swap_sum(far_x, *x) + swap_sum(far_y, *y)
        near = near + swap_sum(near_y, *y) + swap_sum(near_x, *x)
    depth = lax.axis_size("expert")
    total, *column = split(near, depth // 2) + split(far, depth // 2)
    for mask in range(depth - 1, 0, -1):
        total = total + swap_sum(column[mask - 1], "expert", mask)
    return total.astype(jnp.bfloat16)


def load_kernel(source_ref, held_ref, done):
    step = source_ref.shape[1] // COPIES
    copies = [
        pltpu.make_async_copy(
            source_ref.at[expert, pl.ds(part * step, step)],
            held_ref.at[expert, pl.ds(part * step, step)],
            done.at[expert * COPIES + part],
        )
        for expert in range(source_ref.shape[0])
        for part in range(COPIES)
    ]
    for copy in copies:
        copy.start()
    for copy in copies:
        copy.wait()


def hold(weight):
    return pl.pallas_call(
        load_kernel,
        out_shape=pltpu.VMEM(weight.shape, weight.dtype),
        in_specs=[ANYWHERE],
        out_specs=IN_VMEM,
        scratch_shapes=[pltpu.SemaphoreType.DMA((weight.shape[0] * COPIES,))],
        compiler_params=pltpu.CompilerParams(vmem_limit_bytes=1024 * 1024),
        cost_estimate=pl.CostEstimate(
            flops=0, bytes_accessed=2 * weight.size * weight.dtype.itemsize, transcendentals=0
        ),
    )(pltpu.with_memory_space_constraint(weight, pltpu.HBM))


def expert_kernel(exp_dev, picks, parts, *refs):
    pieces, refs = refs[:parts], refs[parts:]
    router_ref, gate_ref, up_ref, down_hbm = refs[:4]
    results, (rows_ref, down_ref, down_done) = refs[4 : 4 + parts], refs[4 + parts :]
    loads = [
        pltpu.make_async_copy(down_hbm.at[local], down_ref.at[local], down_done.at[local])
        for local in range(exp_dev)
    ]
    for load in loads:
        load.start()
    width = down_ref.shape[2]
    spans, start = [], 0
    for piece in pieces:
        spans.append((start, start + piece.shape[0]))
        rows_ref[start : start + piece.shape[0]] = piece[...]
        start += piece.shape[0]
    rows = rows_ref[:, :width]
    ids = rows_ref[:, width:].astype(jnp.float32)
    logits = times_rows(rows, router_ref[...])
    experts = lax.broadcasted_iota(jnp.int32, logits.shape, 1)
    chosen = experts < 0
    for pick in range(picks):
        chosen = jnp.logical_or(chosen, ids[:, pick : pick + 1] == experts.astype(jnp.float32))
    scores = jnp.where(chosen, 1.0 / (1.0 + jnp.exp(-logits)), 0.0)
    mix = scores / jnp.sum(scores, axis=1, keepdims=True)
    first_expert = lax.axis_index("dp") * exp_dev
    hidden, shares = [], []
    for local in range(exp_dev):
        gate = times_rows(gate_ref[local], rows)
        up = times_rows(up_ref[local], rows)
        gated = gate / (1.0 + jnp.exp(-gate)) * up
        hidden.append(gated.T.astype(jnp.bfloat16))
        mine = jnp.where(experts == first_expert + local, mix, 0.0)
        shares.append(jnp.sum(mine, axis=1, keepdims=True))
    for load in loads:
        load.wait()
    block = min(512, width)

    @pl.loop(0, width // block)
    def _(index):
        columns = pl.ds(pl.multiple_of(index * block, block), block)
        total = 0.0
        for local in range(exp_dev):
            out = jnp.dot(
                hidden[local], down_ref[local, :, columns], preferred_element_type=jnp.float32
            )
            total = total + out * shares[local]
        for (start, stop), result in zip(spans, results):
            result[:, columns] = total[start:stop].astype(result.dtype)


def run_experts(pieces, kinds, picks, router, held_gate, held_up, w_down):
    exp_dev, hidden_units, width = w_down.shape
    rows = sum(piece.shape[0] for piece in pieces)
    held = [pltpu.with_memory_space_constraint(w, pltpu.VMEM) for w in (held_gate, held_up)]
    down = pltpu.with_memory_space_constraint(w_down, pltpu.HBM)
    small = rows <= ROWS // 2 or len(pieces) > 1
    return pl.pallas_call(
        functools.partial(expert_kernel, exp_dev, picks, len(pieces)),
        out_shape=[
            (pltpu.VMEM if small else jax.ShapeDtypeStruct)((piece.shape[0], width), kind)
            for piece, kind in zip(pieces, kinds)
        ],
        in_specs=[IN_VMEM] * (len(pieces) + 3) + [ANYWHERE],
        out_specs=[IN_VMEM] * len(pieces),
        scratch_shapes=[
            pltpu.VMEM((rows, pieces[0].shape[1]), jnp.bfloat16),
            pltpu.VMEM(w_down.shape, w_down.dtype),
            pltpu.SemaphoreType.DMA((exp_dev,)),
        ],
        compiler_params=pltpu.CompilerParams(vmem_limit_bytes=VMEM_BYTES),
        cost_estimate=pl.CostEstimate(
            flops=6 * rows * exp_dev * hidden_units * width,
            bytes_accessed=rows * width * 5,
            transcendentals=rows * exp_dev * hidden_units,
        ),
    )(*pieces, router, *held, down)


def body(tokens, expert_ids, router, w_gate, w_up, w_down):
    picks = expert_ids.shape[1]
    tags = jnp.pad(expert_ids.astype(jnp.bfloat16), ((0, 0), (0, LANES - picks)))
    here, there, held_gate, held_up = gather_rows(
        jnp.concatenate([tokens, tags], axis=1), w_gate, w_up
    )
    pieces = here + there
    kinds = [jnp.float32] * len(here) + [jnp.bfloat16] * len(there)
    operands = (picks, router, held_gate, held_up, w_down)
    if sum(piece.shape[0] for piece in pieces) <= ROWS:
        results = run_experts(pieces, kinds, *operands)
    else:
        results = []
        for piece, kind in zip(pieces, kinds):
            chunks = [
                run_experts([piece[start : start + ROWS]], [kind], *operands)[0]
                for start in range(0, piece.shape[0], ROWS)
            ]
            results.append(cat(chunks))
    return scatter_sums(results[: len(here)], results[len(here) :])


def solution(mesh):
    in_specs = (
        P(("dp", "expert"), None),
        P(("dp", "expert"), None),
        P(),
        P("dp", "expert", None),
        P("dp", "expert", None),
        P("dp", "expert", None),
    )
    out_specs = P(("dp", "expert"), None)
    return jax.shard_map(body, mesh=mesh, in_specs=in_specs, out_specs=out_specs, check_vma=False)
```

profile of v0, /device:TPU:0, one launch (start us, length us, event | category | flops | bytes accessed | tf_op | source)
XLA Modules:
  0.0 65.2 jit_solution(17999867998335461287)
XLA Ops:
  0.0 0.7 %convert_element_type.57 = bf16[8,8]{1,0:T(8,128)(2,1)S(1)} convert(s32[8,8]{1,0:T(8,128)} %param.7) | non-fusion elementwise | flops 64 | bytes 384 | tf_op jit(solution)/shard_map/convert_element_type | solution.py:206
  0.7 0.8 %pad_maximum_fusion.2 = bf16[8,4224]{1,0:T(8,128)(2,1)S(1)} fusion(bf16[8,128]{1,0:T(8,128)(2,1)S(1)} %pad.4, bf16[8,4096]{1,0:T(8,128)(2,1)} %param.6), kind=kLoop, calls=%fused_computation.19 | loop fusion | flops 135168 | bytes 135168 | tf_op jit(solution)/shard_map/concatenate | solution.py:208
  1.5 0.0 copy-start.1
  1.5 4.0 %collective-permute-start.1 = (bf16[8,4224]{1,0:T(8,128)(2,1)S(1)}, bf16[8,4224]{1,0:T(8,128)(2,1)S(1)}, u32[]{:S(2)}, u32[]{:S(2)}) collective-permute-start(bf16[8,4224]{1,0:T(8,128)(2,1)S(1)} %pad_maximum_fusion.2), channel_id=1, source_target_pairs={{0,2},{1,3},{2,0},{3,1},{4,6},{5,7},{6,4},{7,5},{8,10},{9,11},{10,... | collective-permute-start | bytes 202760 | tf_op jit(solution)/shard_map/ppermute | solution.py:26
  5.6 1.3 %collective-permute-start.2 = (bf16[8,4224]{1,0:T(8,128)(2,1)S(1)}, bf16[8,4224]{1,0:T(8,128)(2,1)S(1)}, u32[]{:S(2)}, u32[]{:S(2)}) collective-permute-start(bf16[8,4224]{1,0:T(8,128)(2,1)S(1)} %pad_maximum_fusion.2), channel_id=1, source_target_pairs={{0,3},{1,2},{2,1},{3,0},{4,7},{5,6},{6,5},{7,4},{8,11},{9,10},{10,... | collective-permute-start | bytes 202760 | tf_op jit(solution)/shard_map/ppermute | solution.py:26
  6.9 0.2 collective-permute-start
  7.2 2.9 %shard_map.64.refs_7_ = bf16[2,384,4096]{2,1,0:T(8,128)(2,1)S(1)} custom-call(bf16[2,384,4096]{2,1,0:T(8,128)(2,1)} %source_ref.1), custom_call_target="tpu_custom_call" | custom-call | bytes 12582912 | tf_op jit(solution)/shard_map/pallas_call | solution.py:112
  10.0 0.0 collective-permute-done.1
  10.0 1.8 %collective-permute-done.2 = bf16[8,4224]{1,0:T(8,128)(2,1)S(1)} collective-permute-done((bf16[8,4224]{1,0:T(8,128)(2,1)S(1)}, bf16[8,4224]{1,0:T(8,128)(2,1)S(1)}, u32[]{:S(2)}, u32[]{:S(2)}) %collective-permute-start.2) | collective-permute-done | bytes 67616 | tf_op jit(solution)/shard_map/ppermute | solution.py:26
  11.9 1.6 %collective-permute-start.6 = (bf16[16,4224]{1,0:T(8,128)(2,1)S(1)}, bf16[16,4224]{1,0:T(8,128)(2,1)S(1)}, u32[]{:S(2)}, u32[]{:S(2)}) collective-permute-start(bf16[16,4224]{1,0:T(8,128)(2,1)S(1)} %pad_maximum_fusion.1), channel_id=1, source_target_pairs={{0,8},{4,12},{8,0},{12,4},{16,24},{20,28},{24,16},{28,20},{1,9},{5... | collective-permute-start | bytes 405512 | tf_op jit(solution)/shard_map/ppermute | solution.py:26
  13.4 1.5 %collective-permute-start.4 = (bf16[16,4224]{1,0:T(8,128)(2,1)S(1)}, bf16[16,4224]{1,0:T(8,128)(2,1)S(1)}, u32[]{:S(2)}, u32[]{:S(2)}) collective-permute-start(bf16[16,4224]{1,0:T(8,128)(2,1)S(1)} %pad_maximum_fusion.1), channel_id=1, source_target_pairs={{0,16},{4,20},{8,24},{12,28},{16,0},{20,4},{24,8},{28,12},{1,17},{... | collective-permute-start | bytes 405512 | tf_op jit(solution)/shard_map/ppermute | solution.py:26
  15.0 0.0 collective-permute-done
  15.0 0.0 copy-done.1
  15.0 0.6 collective-permute-start.5
  15.5 0.5 collective-permute-start.3
  16.1 0.0 copy-start
  16.1 2.9 %shard_map.65.refs_8_ = bf16[2,384,4096]{2,1,0:T(8,128)(2,1)S(1)} custom-call(bf16[2,384,4096]{2,1,0:T(8,128)(2,1)} %source_ref.2), custom_call_target="tpu_custom_call" | custom-call | bytes 12582912 | tf_op jit(solution)/shard_map/pallas_call | solution.py:112
  19.0 0.1 collective-permute-start.9
  19.1 0.0 collective-permute-done.4
  19.1 1.4 %collective-permute-done.3 = bf16[16,4224]{1,0:T(8,128)(2,1)S(1)} collective-permute-done((bf16[16,4224]{1,0:T(8,128)(2,1)S(1)}, bf16[16,4224]{1,0:T(8,128)(2,1)S(1)}, u32[]{:S(2)}, u32[]{:S(2)}) %collective-permute-start.3) | collective-permute-done | bytes 135200 | tf_op jit(solution)/shard_map/ppermute | solution.py:26
  20.6 1.5 %collective-permute-start.7 = (bf16[16,4224]{1,0:T(8,128)(2,1)S(1)}, bf16[16,4224]{1,0:T(8,128)(2,1)S(1)}, u32[]{:S(2)}, u32[]{:S(2)}) collective-permute-start(bf16[16,4224]{1,0:T(8,128)(2,1)S(1)} %collective-permute-done.3), channel_id=1, source_target_pairs={{0,16},{4,20},{8,24},{12,28},{16,0},{20,4},{24,8},{28,12},{1,17},{... | collective-permute-start | bytes 405512 | tf_op jit(solution)/shard_map/ppermute | solution.py:26
  22.1 0.6 collective-permute-start.8
  22.7 0.0 collective-permute-done.5
  22.7 0.0 collective-permute-done.6
  22.8 0.1 collective-permute-start.10
  22.8 2.7 %collective-permute-done.7 = bf16[16,4224]{1,0:T(8,128)(2,1)S(1)} collective-permute-done((bf16[16,4224]{1,0:T(8,128)(2,1)S(1)}, bf16[16,4224]{1,0:T(8,128)(2,1)S(1)}, u32[]{:S(2)}, u32[]{:S(2)}) %collective-permute-start.7) | collective-permute-done | bytes 135200 | tf_op jit(solution)/shard_map/ppermute | solution.py:26
  25.6 1.6 %collective-permute-done.8 = bf16[16,4224]{1,0:T(8,128)(2,1)S(1)} collective-permute-done((bf16[16,4224]{1,0:T(8,128)(2,1)S(1)}, bf16[16,4224]{1,0:T(8,128)(2,1)S(1)}, u32[]{:S(2)}, u32[]{:S(2)}) %collective-permute-start.8) | collective-permute-done | bytes 135200 | tf_op jit(solution)/shard_map/ppermute | solution.py:26
  27.2 0.1 collective-permute-start.11
  27.3 0.0 collective-permute-done.9.refs_3_
  27.3 1.5 %collective-permute-done.11.refs_5_ = bf16[32,4224]{1,0:T(8,128)(2,1)S(1)} collective-permute-done((bf16[32,4224]{1,0:T(8,128)(2,1)S(1)}, bf16[32,4224]{1,0:T(8,128)(2,1)S(1)}, u32[]{:S(2)}, u32[]{:S(2)}) %collective-permute-start.11) | collective-permute-done | bytes 270368 | tf_op jit(solution)/shard_map/ppermute | solution.py:26
  28.8 0.0 collective-permute-done.10.refs_4_
  28.8 0.0 copy-done
  28.8 10.3 %shard_map.66 = (f32[32,4096]{1,0:T(8,128)S(1)}, f32[64,4096]{1,0:T(8,128)S(1)}, f32[32,4096]{1,0:T(8,128)S(1)}, bf16[32,4096]{1,0:T(8,128)(2,1)S(1)}, bf16[64,4...) custom-call(bf16[32,4224]{1,0:T(8,128)(2,1)S(1)} %constant_dynamic-update-slice_fusion.refs_0_, ...), custom_call_target="tpu_custom_call" | custom-call | flops 4831838208 | bytes 5242880 | tf_op jit(solution)/shard_map/pallas_call | solution.py:182
  39.2 0.2 collective-permute-start.15
  39.4 0.4 collective-permute-start.12
  39.7 0.1 collective-permute-start.13
  39.9 0.9 %collective-permute-done.15 = bf16[32,4096]{1,0:T(8,128)(2,1)S(1)} collective-permute-done((bf16[32,4096]{1,0:T(8,128)(2,1)S(1)}, bf16[32,4096]{1,0:T(8,128)(2,1)S(1)}, u32[]{:S(2)}, u32[]{:S(2)}) %collective-permute-start.15) | collective-permute-done | bytes 262176 | tf_op jit(solution)/shard_map/ppermute | solution.py:26
  40.8 0.1 add_convert_fusion
  40.8 0.8 %collective-permute-start.19 = (bf16[16,4096]{1,0:T(8,128)(2,1)S(1)}, bf16[16,4096]{1,0:T(8,128)(2,1)S(1)}, u32[]{:S(2)}, u32[]{:S(2)}) collective-permute-start(bf16[16,4096]{1,0:T(8,128)(2,1)S(1)} %get-tuple-element.39), channel_id=1, source_target_pairs={{0,8},{4,12},{8,0},{12,4},{16,24},{20,28},{24,16},{28,20},{1,9},{5... | collective-permute-start | bytes 393224 | tf_op jit(solution)/shard_map/ppermute | solution.py:26
  41.6 0.5 collective-permute-start.16
  42.2 0.0 collective-permute-done.13
  42.2 0.1 fusion.8
  42.3 4.2 %collective-permute-done.19 = bf16[16,4096]{1,0:T(8,128)(2,1)S(1)} collective-permute-done((bf16[16,4096]{1,0:T(8,128)(2,1)S(1)}, bf16[16,4096]{1,0:T(8,128)(2,1)S(1)}, u32[]{:S(2)}, u32[]{:S(2)}) %collective-permute-start.19) | collective-permute-done | bytes 131104 | tf_op jit(solution)/shard_map/ppermute | solution.py:26
  46.4 0.5 collective-permute-done.16
  47.0 0.6 collective-permute-start.20
  47.6 1.3 %collective-permute-start.17 = (bf16[16,4096]{1,0:T(8,128)(2,1)S(1)}, bf16[16,4096]{1,0:T(8,128)(2,1)S(1)}, u32[]{:S(2)}, u32[]{:S(2)}) collective-permute-start(bf16[16,4096]{1,0:T(8,128)(2,1)S(1)} %get-tuple-element.34), channel_id=1, source_target_pairs={{0,8},{4,12},{8,0},{12,4},{16,24},{20,28},{24,16},{28,20},{1,9},{5... | collective-permute-start | bytes 393224 | tf_op jit(solution)/shard_map/ppermute | solution.py:26
  48.8 0.7 %collective-permute-start.18 = (bf16[16,4096]{1,0:T(8,128)(2,1)S(1)}, bf16[16,4096]{1,0:T(8,128)(2,1)S(1)}, u32[]{:S(2)}, u32[]{:S(2)}) collective-permute-start(bf16[16,4096]{1,0:T(8,128)(2,1)S(1)} %get-tuple-element.37), channel_id=1, source_target_pairs={{0,8},{4,12},{8,0},{12,4},{16,24},{20,28},{24,16},{28,20},{1,9},{5... | collective-permute-start | bytes 393224 | tf_op jit(solution)/shard_map/ppermute | solution.py:26
  49.6 1.5 %collective-permute-start.14 = (bf16[16,4096]{1,0:T(8,128)(2,1)S(1)}, bf16[16,4096]{1,0:T(8,128)(2,1)S(1)}, u32[]{:S(2)}, u32[]{:S(2)}) collective-permute-start(bf16[16,4096]{1,0:T(8,128)(2,1)S(1)} %get-tuple-element.38), channel_id=1, source_target_pairs={{0,16},{4,20},{8,24},{12,28},{16,0},{20,4},{24,8},{28,12},{1,17},{... | collective-permute-start | bytes 393224 | tf_op jit(solution)/shard_map/ppermute | solution.py:26
  51.1 0.0 collective-permute-done.12
  51.2 2.0 %collective-permute-done.20 = bf16[16,4096]{1,0:T(8,128)(2,1)S(1)} collective-permute-done((bf16[16,4096]{1,0:T(8,128)(2,1)S(1)}, bf16[16,4096]{1,0:T(8,128)(2,1)S(1)}, u32[]{:S(2)}, u32[]{:S(2)}) %collective-permute-start.20) | collective-permute-done | bytes 131104 | tf_op jit(solution)/shard_map/ppermute | solution.py:26
  53.1 0.0 collective-permute-done.17
  53.1 1.3 %collective-permute-done.18 = bf16[16,4096]{1,0:T(8,128)(2,1)S(1)} collective-permute-done((bf16[16,4096]{1,0:T(8,128)(2,1)S(1)}, bf16[16,4096]{1,0:T(8,128)(2,1)S(1)}, u32[]{:S(2)}, u32[]{:S(2)}) %collective-permute-start.18) | collective-permute-done | bytes 131104 | tf_op jit(solution)/shard_map/ppermute | solution.py:26
  54.5 0.1 collective-permute-done.14
  54.6 0.1 fusion.2
  54.7 1.5 %collective-permute-start.23 = (bf16[8,4096]{1,0:T(8,128)(2,1)S(1)}, bf16[8,4096]{1,0:T(8,128)(2,1)S(1)}, u32[]{:S(2)}, u32[]{:S(2)}) collective-permute-start(bf16[8,4096]{1,0:T(8,128)(2,1)S(1)} %slice.89), channel_id=1, source_target_pairs={{0,1},{1,0},{2,3},{3,2},{4,5},{5,4},{6,7},{7,6},{8,9},{9,8},{10,11... | collective-permute-start | bytes 196616 | tf_op jit(solution)/shard_map/ppermute | solution.py:26
  56.2 3.1 %collective-permute-start.21 = (bf16[8,4096]{1,0:T(8,128)(2,1)S(1)}, bf16[8,4096]{1,0:T(8,128)(2,1)S(1)}, u32[]{:S(2)}, u32[]{:S(2)}) collective-permute-start(bf16[8,4096]{1,0:T(8,128)(2,1)S(1)} %get-tuple-element.41), channel_id=1, source_target_pairs={{0,3},{1,2},{2,1},{3,0},{4,7},{5,6},{6,5},{7,4},{8,11},{9,10},{10,... | collective-permute-start | bytes 196616 | tf_op jit(solution)/shard_map/ppermute | solution.py:26
  59.4 0.0 collective-permute-start.22
  59.4 0.0 collective-permute-done.23
  59.4 3.0 %collective-permute-done.21 = bf16[8,4096]{1,0:T(8,128)(2,1)S(1)} collective-permute-done((bf16[8,4096]{1,0:T(8,128)(2,1)S(1)}, bf16[8,4096]{1,0:T(8,128)(2,1)S(1)}, u32[]{:S(2)}, u32[]{:S(2)}) %collective-permute-start.21) | collective-permute-done | bytes 65568 | tf_op jit(solution)/shard_map/ppermute | solution.py:26
  62.4 2.1 %collective-permute-done.22 = bf16[8,4096]{1,0:T(8,128)(2,1)S(1)} collective-permute-done((bf16[8,4096]{1,0:T(8,128)(2,1)S(1)}, bf16[8,4096]{1,0:T(8,128)(2,1)S(1)}, u32[]{:S(2)}, u32[]{:S(2)}) %collective-permute-start.22) | collective-permute-done | bytes 65568 | tf_op jit(solution)/shard_map/ppermute | solution.py:26
  64.5 0.7 %fusion.7 = bf16[8,4096]{1,0:T(8,128)(2,1)} fusion(f32[16,4096]{1,0:T(8,128)S(1)} %get-tuple-element.36, bf16[8,4096]{1,0:T(8,128)(2,1)S(1)} %collective-permute-done.23, bf16[8,4096]{1,0:T(8,128)(2,1)S(1)} %collective-permute-done.22, bf16[8,4096]{1,0:T(8,128)(2,1)S(1)} %collective-permute-done.21), kind=kLoop, calls=%fused_computation.18 | loop fusion | flops 229376 | bytes 393216 | tf_op jit(solution)/shard_map/convert_element_type | solution.py:91
  (17 shorter events, 0.3 us)
Async XLA Ops:
  1.5 13.4 %copy-start.1 = (bf16[8,4096]{1,0:T(8,128)(2,1)S(1)}, bf16[8,4096]{1,0:T(8,128)(2,1)}, u32[]{:S(2)}) copy-start(bf16[8,4096]{1,0:T(8,128)(2,1)} %param.6) | copy-start | bytes 196612
  1.5 8.5 %collective-permute-start.1 = (bf16[8,4224]{1,0:T(8,128)(2,1)S(1)}, bf16[8,4224]{1,0:T(8,128)(2,1)S(1)}, u32[]{:S(2)}, u32[]{:S(2)}) collective-permute-start(bf16[8,4224]{1,0:T(8,128)(2,1)S(1)} %pad_maximum_fusion.2), channel_id=1, source_target_pairs={{0,2},{1,3},{2,0},{3,1},{4,6},{5,7},{6,4},{7,5},{8,10},{9,11},{10,... | collective-permute-start | bytes 202760 | tf_op jit(solution)/shard_map/ppermute | solution.py:26
  5.6 6.3 %collective-permute-start.2 = (bf16[8,4224]{1,0:T(8,128)(2,1)S(1)}, bf16[8,4224]{1,0:T(8,128)(2,1)S(1)}, u32[]{:S(2)}, u32[]{:S(2)}) collective-permute-start(bf16[8,4224]{1,0:T(8,128)(2,1)S(1)} %pad_maximum_fusion.2), channel_id=1, source_target_pairs={{0,3},{1,2},{2,1},{3,0},{4,7},{5,6},{6,5},{7,4},{8,11},{9,10},{10,... | collective-permute-start | bytes 202760 | tf_op jit(solution)/shard_map/ppermute | solution.py:26
  6.9 8.0 %collective-permute-start = (bf16[8,4224]{1,0:T(8,128)(2,1)S(1)}, bf16[8,4224]{1,0:T(8,128)(2,1)S(1)}, u32[]{:S(2)}, u32[]{:S(2)}) collective-permute-start(bf16[8,4224]{1,0:T(8,128)(2,1)S(1)} %pad_maximum_fusion.2), channel_id=1, source_target_pairs={{0,1},{1,0},{2,3},{3,2},{4,5},{5,4},{6,7},{7,6},{8,9},{9,8},{10,11... | collective-permute-start | bytes 202760 | tf_op jit(solution)/shard_map/ppermute | solution.py:26
  11.9 10.8 %collective-permute-start.6 = (bf16[16,4224]{1,0:T(8,128)(2,1)S(1)}, bf16[16,4224]{1,0:T(8,128)(2,1)S(1)}, u32[]{:S(2)}, u32[]{:S(2)}) collective-permute-start(bf16[16,4224]{1,0:T(8,128)(2,1)S(1)} %pad_maximum_fusion.1), channel_id=1, source_target_pairs={{0,8},{4,12},{8,0},{12,4},{16,24},{20,28},{24,16},{28,20},{1,9},{5... | collective-permute-start | bytes 405512 | tf_op jit(solution)/shard_map/ppermute | solution.py:26
  13.4 5.7 %collective-permute-start.4 = (bf16[16,4224]{1,0:T(8,128)(2,1)S(1)}, bf16[16,4224]{1,0:T(8,128)(2,1)S(1)}, u32[]{:S(2)}, u32[]{:S(2)}) collective-permute-start(bf16[16,4224]{1,0:T(8,128)(2,1)S(1)} %pad_maximum_fusion.1), channel_id=1, source_target_pairs={{0,16},{4,20},{8,24},{12,28},{16,0},{20,4},{24,8},{28,12},{1,17},{... | collective-permute-start | bytes 405512 | tf_op jit(solution)/shard_map/ppermute | solution.py:26
  15.0 7.7 %collective-permute-start.5 = (bf16[16,4224]{1,0:T(8,128)(2,1)S(1)}, bf16[16,4224]{1,0:T(8,128)(2,1)S(1)}, u32[]{:S(2)}, u32[]{:S(2)}) collective-permute-start(bf16[16,4224]{1,0:T(8,128)(2,1)S(1)} %pad_maximum_fusion), channel_id=1, source_target_pairs={{0,16},{4,20},{8,24},{12,28},{16,0},{20,4},{24,8},{28,12},{1,17},{... | collective-permute-start | bytes 405512 | tf_op jit(solution)/shard_map/ppermute | solution.py:26
  15.5 5.0 %collective-permute-start.3 = (bf16[16,4224]{1,0:T(8,128)(2,1)S(1)}, bf16[16,4224]{1,0:T(8,128)(2,1)S(1)}, u32[]{:S(2)}, u32[]{:S(2)}) collective-permute-start(bf16[16,4224]{1,0:T(8,128)(2,1)S(1)} %pad_maximum_fusion), channel_id=1, source_target_pairs={{0,8},{4,12},{8,0},{12,4},{16,24},{20,28},{24,16},{28,20},{1,9},{5... | collective-permute-start | bytes 405512 | tf_op jit(solution)/shard_map/ppermute | solution.py:26
  16.1 12.7 %copy-start = (bf16[16,4096]{1,0:T(8,128)(2,1)S(1)}, bf16[16,4096]{1,0:T(8,128)(2,1)}, u32[]{:S(2)}) copy-start(bf16[16,4096]{1,0:T(8,128)(2,1)} %refs_6_.1) | copy-start | bytes 393220
  19.0 8.2 %collective-permute-start.9 = (bf16[32,4224]{1,0:T(8,128)(2,1)S(1)}, bf16[32,4224]{1,0:T(8,128)(2,1)S(1)}, u32[]{:S(2)}, u32[]{:S(2)}) collective-permute-start(bf16[32,4224]{1,0:T(8,128)(2,1)S(1)} %constant_dynamic-update-slice_fusion.refs_0_), channel_id=1, source_target_pairs={{0,4},{4,0},{8,12},{12,8},{16,20},{20,16},{24,28},{28,24},{1,5},{5... | collective-permute-start | bytes 811016 | tf_op jit(solution)/shard_map/ppermute | solution.py:26
  20.6 5.0 %collective-permute-start.7 = (bf16[16,4224]{1,0:T(8,128)(2,1)S(1)}, bf16[16,4224]{1,0:T(8,128)(2,1)S(1)}, u32[]{:S(2)}, u32[]{:S(2)}) collective-permute-start(bf16[16,4224]{1,0:T(8,128)(2,1)S(1)} %collective-permute-done.3), channel_id=1, source_target_pairs={{0,16},{4,20},{8,24},{12,28},{16,0},{20,4},{24,8},{28,12},{1,17},{... | collective-permute-start | bytes 405512 | tf_op jit(solution)/shard_map/ppermute | solution.py:26
  22.1 5.1 %collective-permute-start.8 = (bf16[16,4224]{1,0:T(8,128)(2,1)S(1)}, bf16[16,4224]{1,0:T(8,128)(2,1)S(1)}, u32[]{:S(2)}, u32[]{:S(2)}) collective-permute-start(bf16[16,4224]{1,0:T(8,128)(2,1)S(1)} %collective-permute-done.4), channel_id=1, source_target_pairs={{0,8},{4,12},{8,0},{12,4},{16,24},{20,28},{24,16},{28,20},{1,9},{5... | collective-permute-start | bytes 405512 | tf_op jit(solution)/shard_map/ppermute | solution.py:26
  22.8 6.0 %collective-permute-start.10 = (bf16[64,4224]{1,0:T(8,128)(2,1)S(1)}, bf16[64,4224]{1,0:T(8,128)(2,1)S(1)}, u32[]{:S(2)}, u32[]{:S(2)}) collective-permute-start(bf16[64,4224]{1,0:T(8,128)(2,1)S(1)} %constant_dynamic-update-slice_fusion.2.refs_1_), channel_id=1, source_target_pairs={{0,4},{4,0},{8,12},{12,8},{16,20},{20,16},{24,28},{28,24},{1,5},{5... | collective-permute-start | bytes 1622024 | tf_op jit(solution)/shard_map/ppermute | solution.py:26
  27.2 1.6 %collective-permute-start.11 = (bf16[32,4224]{1,0:T(8,128)(2,1)S(1)}, bf16[32,4224]{1,0:T(8,128)(2,1)S(1)}, u32[]{:S(2)}, u32[]{:S(2)}) collective-permute-start(bf16[32,4224]{1,0:T(8,128)(2,1)S(1)} %constant_dynamic-update-slice_fusion.6.refs_2_), channel_id=1, source_target_pairs={{0,4},{4,0},{8,12},{12,8},{16,20},{20,16},{24,28},{28,24},{1,5},{5... | collective-permute-start | bytes 811016 | tf_op jit(solution)/shard_map/ppermute | solution.py:26
  39.2 1.6 %collective-permute-start.15 = (bf16[32,4096]{1,0:T(8,128)(2,1)S(1)}, bf16[32,4096]{1,0:T(8,128)(2,1)S(1)}, u32[]{:S(2)}, u32[]{:S(2)}) collective-permute-start(bf16[32,4096]{1,0:T(8,128)(2,1)S(1)} %get-tuple-element.30), channel_id=1, source_target_pairs={{0,4},{4,0},{8,12},{12,8},{16,20},{20,16},{24,28},{28,24},{1,5},{5... | collective-permute-start | bytes 786440 | tf_op jit(solution)/shard_map/ppermute | solution.py:26
  39.4 11.8 %collective-permute-start.12 = (bf16[32,4096]{1,0:T(8,128)(2,1)S(1)}, bf16[32,4096]{1,0:T(8,128)(2,1)S(1)}, u32[]{:S(2)}, u32[]{:S(2)}) collective-permute-start(bf16[32,4096]{1,0:T(8,128)(2,1)S(1)} %get-tuple-element.26), channel_id=1, source_target_pairs={{0,4},{4,0},{8,12},{12,8},{16,20},{20,16},{24,28},{28,24},{1,5},{5... | collective-permute-start | bytes 786440 | tf_op jit(solution)/shard_map/ppermute | solution.py:26
  39.7 2.4 %collective-permute-start.13 = (bf16[64,4096]{1,0:T(8,128)(2,1)S(1)}, bf16[64,4096]{1,0:T(8,128)(2,1)S(1)}, u32[]{:S(2)}, u32[]{:S(2)}) collective-permute-start(bf16[64,4096]{1,0:T(8,128)(2,1)S(1)} %get-tuple-element.28), channel_id=1, source_target_pairs={{0,4},{4,0},{8,12},{12,8},{16,20},{20,16},{24,28},{28,24},{1,5},{5... | collective-permute-start | bytes 1572872 | tf_op jit(solution)/shard_map/ppermute | solution.py:26
  40.8 5.6 %collective-permute-start.19 = (bf16[16,4096]{1,0:T(8,128)(2,1)S(1)}, bf16[16,4096]{1,0:T(8,128)(2,1)S(1)}, u32[]{:S(2)}, u32[]{:S(2)}) collective-permute-start(bf16[16,4096]{1,0:T(8,128)(2,1)S(1)} %get-tuple-element.39), channel_id=1, source_target_pairs={{0,8},{4,12},{8,0},{12,4},{16,24},{20,28},{24,16},{28,20},{1,9},{5... | collective-permute-start | bytes 393224 | tf_op jit(solution)/shard_map/ppermute | solution.py:26
  41.6 5.3 %collective-permute-start.16 = (bf16[16,4096]{1,0:T(8,128)(2,1)S(1)}, bf16[16,4096]{1,0:T(8,128)(2,1)S(1)}, u32[]{:S(2)}, u32[]{:S(2)}) collective-permute-start(bf16[16,4096]{1,0:T(8,128)(2,1)S(1)} %get-tuple-element.40), channel_id=1, source_target_pairs={{0,16},{4,20},{8,24},{12,28},{16,0},{20,4},{24,8},{28,12},{1,17},{... | collective-permute-start | bytes 393224 | tf_op jit(solution)/shard_map/ppermute | solution.py:26
  47.0 6.1 %collective-permute-start.20 = (bf16[16,4096]{1,0:T(8,128)(2,1)S(1)}, bf16[16,4096]{1,0:T(8,128)(2,1)S(1)}, u32[]{:S(2)}, u32[]{:S(2)}) collective-permute-start(bf16[16,4096]{1,0:T(8,128)(2,1)S(1)} %get-tuple-element.33), channel_id=1, source_target_pairs={{0,16},{4,20},{8,24},{12,28},{16,0},{20,4},{24,8},{28,12},{1,17},{... | collective-permute-start | bytes 393224 | tf_op jit(solution)/shard_map/ppermute | solution.py:26
  47.6 5.6 %collective-permute-start.17 = (bf16[16,4096]{1,0:T(8,128)(2,1)S(1)}, bf16[16,4096]{1,0:T(8,128)(2,1)S(1)}, u32[]{:S(2)}, u32[]{:S(2)}) collective-permute-start(bf16[16,4096]{1,0:T(8,128)(2,1)S(1)} %get-tuple-element.34), channel_id=1, source_target_pairs={{0,8},{4,12},{8,0},{12,4},{16,24},{20,28},{24,16},{28,20},{1,9},{5... | collective-permute-start | bytes 393224 | tf_op jit(solution)/shard_map/ppermute | solution.py:26
  48.8 5.6 %collective-permute-start.18 = (bf16[16,4096]{1,0:T(8,128)(2,1)S(1)}, bf16[16,4096]{1,0:T(8,128)(2,1)S(1)}, u32[]{:S(2)}, u32[]{:S(2)}) collective-permute-start(bf16[16,4096]{1,0:T(8,128)(2,1)S(1)} %get-tuple-element.37), channel_id=1, source_target_pairs={{0,8},{4,12},{8,0},{12,4},{16,24},{20,28},{24,16},{28,20},{1,9},{5... | collective-permute-start | bytes 393224 | tf_op jit(solution)/shard_map/ppermute | solution.py:26
  49.6 5.0 %collective-permute-start.14 = (bf16[16,4096]{1,0:T(8,128)(2,1)S(1)}, bf16[16,4096]{1,0:T(8,128)(2,1)S(1)}, u32[]{:S(2)}, u32[]{:S(2)}) collective-permute-start(bf16[16,4096]{1,0:T(8,128)(2,1)S(1)} %get-tuple-element.38), channel_id=1, source_target_pairs={{0,16},{4,20},{8,24},{12,28},{16,0},{20,4},{24,8},{28,12},{1,17},{... | collective-permute-start | bytes 393224 | tf_op jit(solution)/shard_map/ppermute | solution.py:26
  54.7 4.7 %collective-permute-start.23 = (bf16[8,4096]{1,0:T(8,128)(2,1)S(1)}, bf16[8,4096]{1,0:T(8,128)(2,1)S(1)}, u32[]{:S(2)}, u32[]{:S(2)}) collective-permute-start(bf16[8,4096]{1,0:T(8,128)(2,1)S(1)} %slice.89), channel_id=1, source_target_pairs={{0,1},{1,0},{2,3},{3,2},{4,5},{5,4},{6,7},{7,6},{8,9},{9,8},{10,11... | collective-permute-start | bytes 196616 | tf_op jit(solution)/shard_map/ppermute | solution.py:26
  56.2 6.2 %collective-permute-start.21 = (bf16[8,4096]{1,0:T(8,128)(2,1)S(1)}, bf16[8,4096]{1,0:T(8,128)(2,1)S(1)}, u32[]{:S(2)}, u32[]{:S(2)}) collective-permute-start(bf16[8,4096]{1,0:T(8,128)(2,1)S(1)} %get-tuple-element.41), channel_id=1, source_target_pairs={{0,3},{1,2},{2,1},{3,0},{4,7},{5,6},{6,5},{7,4},{8,11},{9,10},{10,... | collective-permute-start | bytes 196616 | tf_op jit(solution)/shard_map/ppermute | solution.py:26
  59.4 5.2 %collective-permute-start.22 = (bf16[8,4096]{1,0:T(8,128)(2,1)S(1)}, bf16[8,4096]{1,0:T(8,128)(2,1)S(1)}, u32[]{:S(2)}, u32[]{:S(2)}) collective-permute-start(bf16[8,4096]{1,0:T(8,128)(2,1)S(1)} %get-tuple-element.42), channel_id=1, source_target_pairs={{0,2},{1,3},{2,0},{3,1},{4,6},{5,7},{6,4},{7,5},{8,10},{9,11},{10,... | collective-permute-start | bytes 196616 | tf_op jit(solution)/shard_map/ppermute | solution.py:26
where the time goes:
time: 65.4 us; the launch traced here: 65.2 us
  waiting for transfers between devices  23.2 us (35%)
  starting transfers between devices  22.9 us (35%)
  Pallas kernels  16.1 us (25%)
  other arithmetic  2.6 us (4%)
    ppermute x24, waiting for transfers between devices, swap(): return lax.ppermute(value, axis, [(i, i ^ mask) for i in range(count)])  23.2 us
    ppermute x24, starting transfers between devices, swap(): return lax.ppermute(value, axis, [(i, i ^ mask) for i in range(count)])  22.9 us
    pallas_call x1, Pallas kernels, run_experts(): pl.pallas_call(functools.partial(expert_kernel, exp_dev, picks, len(piece...  10.3 us
    pallas_call x2, Pallas kernels, hold(): pl.pallas_call(load_kernel, out_shape=pltpu.VMEM(weight.shape, weight.dty...  5.75 us
  transfers between devices with their start and end apart: 24, of which 13 were waited for; matrix products, arithmetic and copies ran while one was open for 1% of the time, Pallas kernels for 9%

commit v1 on v0

v1 whole, which is shorter than its diff:
```python
import functools

import jax
import jax.numpy as jnp
from jax import lax
from jax.experimental import pallas as pl
from jax.experimental.pallas import tpu as pltpu
from jax.sharding import PartitionSpec as P

LANES = 128
ROWS = 256
COPIES = 4
TERMS = 3
VMEM_BYTES = 36 * 1024 * 1024
IN_VMEM = pl.BlockSpec(memory_space=pltpu.VMEM)
ANYWHERE = pl.BlockSpec(memory_space=pl.ANY)


def times_rows(left, right):
    return lax.dot_general(
        left, right, (((1,), (1,)), ((), ())), preferred_element_type=jnp.float32
    )


def swap(value, axis, mask):
    count = lax.axis_size(axis)
    return lax.ppermute(value, axis, [(i, i ^ mask) for i in range(count)])


def send(value, step):
    return swap(value.astype(jnp.bfloat16), *step)


def wide(value):
    return value.astype(jnp.float32)


def squares():
    plane = [1 << bit for bit in range(1, lax.axis_size("dp").bit_length() - 1)]
    x_masks, y_masks = plane[: len(plane) // 2], plane[len(plane) // 2 :]
    return [(("dp", x), ("dp", y)) for x, y in zip(x_masks, y_masks)]


CORE = ("dp", 1)


def cat(parts):
    return parts[0] if len(parts) == 1 else jnp.concatenate(parts)


def split(value, count):
    step = value.shape[0] // count
    return [value[start : start + step] for start in range(0, value.shape[0], step)]


def gather_rows(block, loads):
    depth = lax.axis_size("expert")
    column = [block] + [swap(block, "expert", mask) for mask in range(1, depth)]
    near = cat(column[: depth // 2])
    near, *column = lax.optimization_barrier((near, *column[depth // 2 :]))
    far = cat(column)
    held = [hold(*loads[0])]
    far, *held = lax.optimization_barrier((far, *held))
    levels = squares()
    for level, (x, y) in enumerate(levels):
        near_x, near_y = swap(near, *x), swap(near, *y)
        far_x, far_y = swap(far, *x), swap(far, *y)
        if level == 0:
            expert, *weights = loads[1]
            near_x, *weights = lax.optimization_barrier((near_x, *weights))
            far_y, *held = lax.optimization_barrier((far_y, *held, hold(expert, *weights)))
        near_d, far_d = swap(near_x, *y), swap(far_y, *x)
        if level < len(levels) - 1:
            near, far = cat([near, near_x, near_y, near_d]), cat([far, far_x, far_y, far_d])
    groups = [cat([near, far]), cat([near_x, near_y, far_x, far_y]), cat([near_d, far_d])]
    return groups, [swap(group, *CORE) for group in groups], held


def scatter_sums(kept, away):
    def joined(index):
        return kept[index] + swap(away[index], *CORE).astype(jnp.float32)

    near_d, far_d = split(joined(2), 2)
    near_x, near_y, far_x, far_y = split(joined(1), 4)
    near, far = split(joined(0), 2)
    levels = squares()[::-1]
    for level, (x, y) in enumerate(levels):
        if level > 0:
            near, near_x, near_y, near_d = split(near, 4)
            far, far_x, far_y, far_d = split(far, 4)
        far_d_here, far_x_here = send(far_d, x), send(far_x, x)
        near_d_here, near_y_here = send(near_d, y), send(near_y, y)
        far_y_here = send(far_y + wide(far_d_here), y)
        near_x_here = send(near_x + wide(near_d_here), x)
        far = far + wide(far_x_here) + wide(far_y_here)
        far, near_x_here, near_y_here = lax.optimization_barrier((far, near_x_here, near_y_here))
        near = near + wide(near_y_here) + wide(near_x_here)
    depth = lax.axis_size("expert")
    total, *column = split(near, depth // 2) + split(far, depth // 2)
    for mask in range(depth - 1, 0, -1):
        total = total + wide(send(column[mask - 1], ("expert", mask)))
    return total.astype(jnp.bfloat16)


def pack_kernel(tokens_hbm, ids_hbm, router_hbm, packed_ref, tokens_ref, ids_ref, router_ref, done):
    pairs = [(tokens_hbm, tokens_ref), (ids_hbm, ids_ref), (router_hbm, router_ref)]
    copies = [
        pltpu.make_async_copy(source, target, done.at[index])
        for index, (source, target) in enumerate(pairs)
    ]
    for copy in copies:
        copy.start()
    for copy in copies:
        copy.wait()
    tokens = tokens_ref[...]
    width, expert_total = tokens.shape[1], router_ref.shape[0]
    logits = times_rows(tokens, router_ref[...])
    experts = lax.broadcasted_iota(jnp.int32, logits.shape, 1)
    ids = ids_ref[...]
    chosen = experts < 0
    for pick in range(ids.shape[1]):
        chosen = jnp.logical_or(chosen, ids[:, pick : pick + 1] == experts)
    scores = jnp.where(chosen, 1.0 / (1.0 + jnp.exp(-logits)), 0.0)
    rest = scores / jnp.sum(scores, axis=1, keepdims=True)
    place = (expert_total, packed_ref.shape[1] - width)
    source, lane = [lax.broadcasted_iota(jnp.int32, place, axis) for axis in (0, 1)]
    tags = 0.0
    for term in range(TERMS):
        part = rest.astype(jnp.bfloat16)
        rest = rest - part.astype(jnp.float32)
        moved = (lane == source + term * expert_total).astype(jnp.float32).astype(jnp.bfloat16)
        tags = tags + jnp.dot(part, moved, preferred_element_type=jnp.float32)
    packed_ref[:, :width] = tokens
    packed_ref[:, width:] = tags.astype(jnp.bfloat16)


def pack(tokens, expert_ids, router):
    rows, width = tokens.shape
    extra = -(-TERMS * router.shape[0] // LANES) * LANES
    return pl.pallas_call(
        pack_kernel,
        out_shape=pltpu.VMEM((rows, width + extra), tokens.dtype),
        in_specs=[ANYWHERE] * 3,
        out_specs=IN_VMEM,
        scratch_shapes=[
            *[pltpu.VMEM(value.shape, value.dtype) for value in (tokens, expert_ids, router)],
            pltpu.SemaphoreType.DMA((3,)),
        ],
        cost_estimate=pl.CostEstimate(
            flops=2 * rows * router.size, bytes_accessed=4 * router.size, transcendentals=0
        ),
    )(*[pltpu.with_memory_space_constraint(v, pltpu.HBM) for v in (tokens, expert_ids, router)])


def load_kernel(expert, *refs):
    *sources, held_ref, done = refs
    units = sources[0].shape[1]
    step = units // COPIES
    copies = [
        pltpu.make_async_copy(
            source.at[expert, pl.ds(part * step, step)],
            held_ref.at[pl.ds(index * units + part * step, step)],
            done.at[index * COPIES + part],
        )
        for index, source in enumerate(sources)
        for part in range(COPIES)
    ]
    for copy in copies:
        copy.start()
    for copy in copies:
        copy.wait()


def hold(expert, *weights):
    _, units, width = weights[0].shape
    return pl.pallas_call(
        functools.partial(load_kernel, expert),
        out_shape=pltpu.VMEM((len(weights) * units, width), weights[0].dtype),
        in_specs=[ANYWHERE] * len(weights),
        out_specs=IN_VMEM,
        scratch_shapes=[pltpu.SemaphoreType.DMA((len(weights) * COPIES,))],
        compiler_params=pltpu.CompilerParams(vmem_limit_bytes=1024 * 1024),
        cost_estimate=pl.CostEstimate(flops=0, bytes_accessed=0, transcendentals=0),
    )(*[pltpu.with_memory_space_constraint(weight, pltpu.HBM) for weight in weights])


def expert_kernel(exp_dev, expert_total, parts, *refs):
    pieces, refs = refs[:parts], refs[parts:]
    held, down_hbm, refs = refs[:exp_dev], refs[exp_dev], refs[exp_dev + 1 :]
    results, (rows_ref, down_ref, down_done) = refs[:parts], refs[parts:]
    units, width = down_ref.shape[1:]
    step = units // COPIES
    loads = [
        pltpu.make_async_copy(
            down_hbm.at[local, pl.ds(part * step, step)],
            down_ref.at[local, pl.ds(part * step, step)],
            down_done.at[local * COPIES + part],
        )
        for local in range(exp_dev)
        for part in range(COPIES)
    ]
    for load in loads:
        load.start()
    spans, start = [], 0
    for piece in pieces:
        spans.append((start, start + piece.shape[0]))
        rows_ref[start : start + piece.shape[0]] = piece[...]
        start += piece.shape[0]
    tags = rows_ref[:, width:].astype(jnp.float32)
    lane = lax.rem(lax.broadcasted_iota(jnp.int32, tags.shape, 1), expert_total)
    first_expert = lax.axis_index("dp") * exp_dev
    hidden, shares = [], []
    for local in range(exp_dev):
        both = times_rows(held[local][...], rows_ref[:, :width])
        gate, up = both[:units], both[units:]
        gated = gate / (1.0 + jnp.exp(-gate)) * up
        hidden.append(gated.T.astype(jnp.bfloat16))
        mine = jnp.where(lane == first_expert + local, tags, 0.0)
        shares.append(jnp.sum(mine, axis=1, keepdims=True))
    for load in loads:
        load.wait()
    block = min(512, width)

    @pl.loop(0, width // block)
    def _(index):
        columns = pl.ds(pl.multiple_of(index * block, block), block)
        total = 0.0
        for local in range(exp_dev):
            out = jnp.dot(
                hidden[local], down_ref[local, :, columns], preferred_element_type=jnp.float32
            )
            total = total + out * shares[local]
        for (start, stop), result in zip(spans, results):
            result[:, columns] = total[start:stop].astype(result.dtype)


def run_experts(pieces, kinds, expert_total, held, w_down):
    exp_dev, units, width = w_down.shape
    rows = sum(piece.shape[0] for piece in pieces)
    held = [pltpu.with_memory_space_constraint(weight, pltpu.VMEM) for weight in held]
    down = pltpu.with_memory_space_constraint(w_down, pltpu.HBM)
    place = pltpu.VMEM if len(pieces) > 1 else jax.ShapeDtypeStruct
    return pl.pallas_call(
        functools.partial(expert_kernel, exp_dev, expert_total, len(pieces)),
        out_shape=[
            place((piece.shape[0], width), kind) for piece, kind in zip(pieces, kinds)
        ],
        in_specs=[IN_VMEM] * (len(pieces) + exp_dev) + [ANYWHERE],
        out_specs=[IN_VMEM] * len(pieces),
        scratch_shapes=[
            pltpu.VMEM((rows, pieces[0].shape[1]), jnp.bfloat16),
            pltpu.VMEM(w_down.shape, w_down.dtype),
            pltpu.SemaphoreType.DMA((exp_dev * COPIES,)),
        ],
        compiler_params=pltpu.CompilerParams(vmem_limit_bytes=VMEM_BYTES),
        cost_estimate=pl.CostEstimate(
            flops=6 * rows * exp_dev * units * width,
            bytes_accessed=rows * width * 5,
            transcendentals=rows * exp_dev * units,
        ),
    )(*pieces, *held, down)


def body(tokens, expert_ids, router, w_gate, w_up, w_down):
    loads = [(expert, w_gate, w_up) for expert in range(w_gate.shape[0])]
    here, there, held = gather_rows(pack(tokens, expert_ids, router), loads)
    pieces = here + there
    kinds = [jnp.float32] * len(here) + [jnp.bfloat16] * len(there)
    operands = (router.shape[0], held, w_down)
    if sum(piece.shape[0] for piece in pieces) <= ROWS:
        results = run_experts(pieces, kinds, *operands)
    else:
        results = []
        for piece, kind in zip(pieces, kinds):
            chunks = [
                run_experts([piece[start : start + ROWS]], [kind], *operands)[0]
                for start in range(0, piece.shape[0], ROWS)
            ]
            results.append(cat(chunks))
    return scatter_sums(results[: len(here)], results[len(here) :])


def solution(mesh):
    in_specs = (
        P(("dp", "expert"), None),
        P(("dp", "expert"), None),
        P(),
        P("dp", "expert", None),
        P("dp", "expert", None),
        P("dp", "expert", None),
    )
    out_specs = P(("dp", "expert"), None)
    return jax.shard_map(body, mesh=mesh, in_specs=in_specs, out_specs=out_specs, check_vma=False)
```

time: 65.4 us -> 67.2 us (1.028)
  other arithmetic: 2.6 us -> 1.05 us
  waiting for transfers between devices: 23.2 us -> 24.5 us
  starting transfers between devices: 22.9 us -> 24.1 us
  Pallas kernels: 16.1 us -> 17 us
    ppermute x24, waiting for transfers between devices: 23.2 us -> 24.5 us  [swap(): return lax.ppermute(value, axis, [(i, i ^ mask) for i in range(count)])]
    ppermute x24, starting transfers between devices: 22.9 us -> 24.1 us  [swap(): return lax.ppermute(value, axis, [(i, i ^ mask) for i in range(count)])]
    pallas_call x3 -> x4, Pallas kernels: 16.1 us -> 17 us  [the longest x1 9.89 us: run_experts(): pl.pallas_call(functools.partial(expert_kernel, exp_dev, expert_total, le...]
    concatenate x1 -> x0, other arithmetic: 0.84 us -> none  [body(): jnp.concatenate([tokens, tags], axis=1)]
    convert_element_type x2 -> x1, other arithmetic: 0.74 us -> 0.05 us  [send(): return swap(value.astype(jnp.bfloat16), *step)]
  transfers between devices with their start and end apart: 24 -> 24, of which waited for: 13 -> 14; matrix products, arithmetic and copies ran while one was open for 1% -> 1% of each run, Pallas kernels for 9% -> 9%
where the time goes in v1:
time: 67.2 us; the launch traced here: 67.1 us
  waiting for transfers between devices  24.5 us (36%)
  starting transfers between devices  24.1 us (36%)
  Pallas kernels  17 us (25%)
  other arithmetic  1.05 us (2%)
    ppermute x24, waiting for transfers between devices, swap(): return lax.ppermute(value, axis, [(i, i ^ mask) for i in range(count)])  24.5 us
    ppermute x24, starting transfers between devices, swap(): return lax.ppermute(value, axis, [(i, i ^ mask) for i in range(count)])  24.1 us
    pallas_call x1, Pallas kernels, run_experts(): pl.pallas_call(functools.partial(expert_kernel, exp_dev, expert_total, le...  9.89 us
    pallas_call x2, Pallas kernels, hold(): pl.pallas_call(functools.partial(load_kernel, expert), out_shape=pltpu.VM...  5.72 us
    pallas_call x1, Pallas kernels, pack(): pl.pallas_call(pack_kernel, out_shape=pltpu.VMEM((rows, width + extra), t...  1.4 us
  transfers between devices with their start and end apart: 24, of which 14 were waited for; matrix products, arithmetic and copies ran while one was open for 1% of the time, Pallas kernels for 9%

profile of v1, /device:TPU:0, one launch (start us, length us, event | category | flops | bytes accessed | tf_op | source)
XLA Modules:
  0.0 67.1 jit_solution(3102287452588359117)
XLA Ops:
  0.0 1.4 %shard_map.64 = bf16[8,4224]{1,0:T(8,128)(2,1)S(1)} custom-call(bf16[8,4096]{1,0:T(8,128)(2,1)} %tokens_hbm.1, s32[8,8]{1,0:T(8,128)} %ids_hbm.1, bf16[16,4096]{1,0:T(8,128)(2,1)} %router_hbm.1), custom_call_target="tpu_custom_call" | custom-call | flops 1048576 | bytes 262144 | tf_op jit(solution)/shard_map/pallas_call | solution.py:140
  1.4 3.1 %collective-permute-start = (bf16[8,4224]{1,0:T(8,128)(2,1)S(1)}, bf16[8,4224]{1,0:T(8,128)(2,1)S(1)}, u32[]{:S(2)}, u32[]{:S(2)}) collective-permute-start(bf16[8,4224]{1,0:T(8,128)(2,1)S(1)} %shard_map.64), channel_id=1, source_target_pairs={{0,1},{1,0},{2,3},{3,2},{4,5},{5,4},{6,7},{7,6},{8,9},{9,8},{10,11... | collective-permute-start | bytes 202760 | tf_op jit(solution)/shard_map/ppermute | solution.py:27
  4.5 2.5 %collective-permute-start.2 = (bf16[8,4224]{1,0:T(8,128)(2,1)S(1)}, bf16[8,4224]{1,0:T(8,128)(2,1)S(1)}, u32[]{:S(2)}, u32[]{:S(2)}) collective-permute-start(bf16[8,4224]{1,0:T(8,128)(2,1)S(1)} %shard_map.64), channel_id=1, source_target_pairs={{0,3},{1,2},{2,1},{3,0},{4,7},{5,6},{6,5},{7,4},{8,11},{9,10},{10,... | collective-permute-start | bytes 202760 | tf_op jit(solution)/shard_map/ppermute | solution.py:27
  7.0 0.1 collective-permute-start.1
  7.1 2.9 %shard_map.65.refs_6_ = bf16[768,4096]{1,0:T(8,128)(2,1)S(1)} custom-call(bf16[2,384,4096]{2,1,0:T(8,128)(2,1)} %refs_0_.2, bf16[2,384,4096]{2,1,0:T(8,128)(2,1)} %refs_1_.2), custom_call_target="tpu_custom_call" | custom-call | tf_op jit(solution)/shard_map/pallas_call | solution.py:176
  10.0 0.0 collective-permute-done
  10.0 1.4 %collective-permute-done.2 = bf16[8,4224]{1,0:T(8,128)(2,1)S(1)} collective-permute-done((bf16[8,4224]{1,0:T(8,128)(2,1)S(1)}, bf16[8,4224]{1,0:T(8,128)(2,1)S(1)}, u32[]{:S(2)}, u32[]{:S(2)}) %collective-permute-start.2) | collective-permute-done | bytes 67616 | tf_op jit(solution)/shard_map/ppermute | solution.py:27
  11.4 2.1 %collective-permute-done.1 = bf16[8,4224]{1,0:T(8,128)(2,1)S(1)} collective-permute-done((bf16[8,4224]{1,0:T(8,128)(2,1)S(1)}, bf16[8,4224]{1,0:T(8,128)(2,1)S(1)}, u32[]{:S(2)}, u32[]{:S(2)}) %collective-permute-start.1) | collective-permute-done | bytes 67616 | tf_op jit(solution)/shard_map/ppermute | solution.py:27
  13.6 1.5 %collective-permute-start.4 = (bf16[16,4224]{1,0:T(8,128)(2,1)S(1)}, bf16[16,4224]{1,0:T(8,128)(2,1)S(1)}, u32[]{:S(2)}, u32[]{:S(2)}) collective-permute-start(bf16[16,4224]{1,0:T(8,128)(2,1)S(1)} %pad_maximum_fusion), channel_id=1, source_target_pairs={{0,16},{4,20},{8,24},{12,28},{16,0},{20,4},{24,8},{28,12},{1,17},{... | collective-permute-start | bytes 405512 | tf_op jit(solution)/shard_map/ppermute | solution.py:27
  15.1 1.5 %collective-permute-start.3 = (bf16[16,4224]{1,0:T(8,128)(2,1)S(1)}, bf16[16,4224]{1,0:T(8,128)(2,1)S(1)}, u32[]{:S(2)}, u32[]{:S(2)}) collective-permute-start(bf16[16,4224]{1,0:T(8,128)(2,1)S(1)} %pad_maximum_fusion), channel_id=1, source_target_pairs={{0,8},{4,12},{8,0},{12,4},{16,24},{20,28},{24,16},{28,20},{1,9},{5... | collective-permute-start | bytes 405512 | tf_op jit(solution)/shard_map/ppermute | solution.py:27
  16.6 0.6 collective-permute-start.6
  17.2 0.5 collective-permute-start.5
  17.7 0.1 collective-permute-start.9
  17.8 3.8 %collective-permute-done.3 = bf16[16,4224]{1,0:T(8,128)(2,1)S(1)} collective-permute-done((bf16[16,4224]{1,0:T(8,128)(2,1)S(1)}, bf16[16,4224]{1,0:T(8,128)(2,1)S(1)}, u32[]{:S(2)}, u32[]{:S(2)}) %collective-permute-start.3) | collective-permute-done | bytes 135200 | tf_op jit(solution)/shard_map/ppermute | solution.py:27
  21.6 0.0 collective-permute-start.7
  21.6 2.9 %shard_map.66.refs_7_ = bf16[768,4096]{1,0:T(8,128)(2,1)S(1)} custom-call(bf16[2,384,4096]{2,1,0:T(8,128)(2,1)} %refs_0_.2, bf16[2,384,4096]{2,1,0:T(8,128)(2,1)} %refs_1_.2), custom_call_target="tpu_custom_call" | custom-call | tf_op jit(solution)/shard_map/pallas_call | solution.py:176
  24.5 0.0 collective-permute-done.6
  24.5 2.0 %collective-permute-start.8 = (bf16[16,4224]{1,0:T(8,128)(2,1)S(1)}, bf16[16,4224]{1,0:T(8,128)(2,1)S(1)}, u32[]{:S(2)}, u32[]{:S(2)}) collective-permute-start(bf16[16,4224]{1,0:T(8,128)(2,1)S(1)} %collective-permute-done.6), channel_id=1, source_target_pairs={{0,8},{4,12},{8,0},{12,4},{16,24},{20,28},{24,16},{28,20},{1,9},{5... | collective-permute-start | bytes 405512 | tf_op jit(solution)/shard_map/ppermute | solution.py:27
  26.5 0.0 collective-permute-done.4
  26.5 0.0 collective-permute-done.5
  26.6 0.1 collective-permute-start.10
  26.7 0.0 collective-permute-done.7
  26.7 2.9 %collective-permute-done.8 = bf16[16,4224]{1,0:T(8,128)(2,1)S(1)} collective-permute-done((bf16[16,4224]{1,0:T(8,128)(2,1)S(1)}, bf16[16,4224]{1,0:T(8,128)(2,1)S(1)}, u32[]{:S(2)}, u32[]{:S(2)}) %collective-permute-start.8) | collective-permute-done | bytes 135200 | tf_op jit(solution)/shard_map/ppermute | solution.py:27
  29.6 0.1 collective-permute-start.11
  29.7 0.0 collective-permute-done.9.refs_3_
  29.7 1.5 %collective-permute-done.11.refs_5_ = bf16[32,4224]{1,0:T(8,128)(2,1)S(1)} collective-permute-done((bf16[32,4224]{1,0:T(8,128)(2,1)S(1)}, bf16[32,4224]{1,0:T(8,128)(2,1)S(1)}, u32[]{:S(2)}, u32[]{:S(2)}) %collective-permute-start.11) | collective-permute-done | bytes 270368 | tf_op jit(solution)/shard_map/ppermute | solution.py:27
  31.2 0.0 collective-permute-done.10.refs_4_
  31.2 9.9 %shard_map.67 = (f32[32,4096]{1,0:T(8,128)S(1)}, f32[64,4096]{1,0:T(8,128)S(1)}, f32[32,4096]{1,0:T(8,128)S(1)}, bf16[32,4096]{1,0:T(8,128)(2,1)S(1)}, bf16[64,4...) custom-call(bf16[32,4224]{1,0:T(8,128)(2,1)S(1)} %constant_dynamic-update-slice_fusion.refs_0_, ...), custom_call_target="tpu_custom_call" | custom-call | flops 4831838208 | bytes 5242880 | tf_op jit(solution)/shard_map/pallas_call | solution.py:243
  41.1 0.2 collective-permute-start.15
  41.3 0.4 collective-permute-start.12
  41.7 0.1 collective-permute-start.13
  41.8 0.9 %collective-permute-done.15 = bf16[32,4096]{1,0:T(8,128)(2,1)S(1)} collective-permute-done((bf16[32,4096]{1,0:T(8,128)(2,1)S(1)}, bf16[32,4096]{1,0:T(8,128)(2,1)S(1)}, u32[]{:S(2)}, u32[]{:S(2)}) %collective-permute-start.15) | collective-permute-done | bytes 262176 | tf_op jit(solution)/shard_map/ppermute | solution.py:27
  42.7 0.1 add_convert_fusion
  42.8 2.1 %collective-permute-start.18 = (bf16[16,4096]{1,0:T(8,128)(2,1)S(1)}, bf16[16,4096]{1,0:T(8,128)(2,1)S(1)}, u32[]{:S(2)}, u32[]{:S(2)}) collective-permute-start(bf16[16,4096]{1,0:T(8,128)(2,1)S(1)} %get-tuple-element.51), channel_id=1, source_target_pairs={{0,16},{4,20},{8,24},{12,28},{16,0},{20,4},{24,8},{28,12},{1,17},{... | collective-permute-start | bytes 393224 | tf_op jit(solution)/shard_map/ppermute | solution.py:27
  44.9 1.5 %collective-permute-start.16 = (bf16[16,4096]{1,0:T(8,128)(2,1)S(1)}, bf16[16,4096]{1,0:T(8,128)(2,1)S(1)}, u32[]{:S(2)}, u32[]{:S(2)}) collective-permute-start(bf16[16,4096]{1,0:T(8,128)(2,1)S(1)} %get-tuple-element.52), channel_id=1, source_target_pairs={{0,8},{4,12},{8,0},{12,4},{16,24},{20,28},{24,16},{28,20},{1,9},{5... | collective-permute-start | bytes 393224 | tf_op jit(solution)/shard_map/ppermute | solution.py:27
  46.3 0.0 collective-permute-done.13
  46.3 0.1 fusion.7
  46.5 2.2 %collective-permute-done.18 = bf16[16,4096]{1,0:T(8,128)(2,1)S(1)} collective-permute-done((bf16[16,4096]{1,0:T(8,128)(2,1)S(1)}, bf16[16,4096]{1,0:T(8,128)(2,1)S(1)}, u32[]{:S(2)}, u32[]{:S(2)}) %collective-permute-start.18) | collective-permute-done | bytes 131104 | tf_op jit(solution)/shard_map/ppermute | solution.py:27
  48.7 1.5 %collective-permute-done.16 = bf16[16,4096]{1,0:T(8,128)(2,1)S(1)} collective-permute-done((bf16[16,4096]{1,0:T(8,128)(2,1)S(1)}, bf16[16,4096]{1,0:T(8,128)(2,1)S(1)}, u32[]{:S(2)}, u32[]{:S(2)}) %collective-permute-start.16) | collective-permute-done | bytes 131104 | tf_op jit(solution)/shard_map/ppermute | solution.py:27
  50.2 0.4 collective-permute-start.17
  50.6 1.6 %collective-permute-start.14 = (bf16[16,4096]{1,0:T(8,128)(2,1)S(1)}, bf16[16,4096]{1,0:T(8,128)(2,1)S(1)}, u32[]{:S(2)}, u32[]{:S(2)}) collective-permute-start(bf16[16,4096]{1,0:T(8,128)(2,1)S(1)} %get-tuple-element.50), channel_id=1, source_target_pairs={{0,8},{4,12},{8,0},{12,4},{16,24},{20,28},{24,16},{28,20},{1,9},{5... | collective-permute-start | bytes 393224 | tf_op jit(solution)/shard_map/ppermute | solution.py:27
  52.2 0.0 collective-permute-done.12
  52.3 0.5 collective-permute-start.19
  52.8 1.7 %collective-permute-start.20 = (bf16[16,4096]{1,0:T(8,128)(2,1)S(1)}, bf16[16,4096]{1,0:T(8,128)(2,1)S(1)}, u32[]{:S(2)}, u32[]{:S(2)}) collective-permute-start(bf16[16,4096]{1,0:T(8,128)(2,1)S(1)} %get-tuple-element.49), channel_id=1, source_target_pairs={{0,16},{4,20},{8,24},{12,28},{16,0},{20,4},{24,8},{28,12},{1,17},{... | collective-permute-start | bytes 393224 | tf_op jit(solution)/shard_map/ppermute | solution.py:27
  54.4 2.2 %collective-permute-done.17 = bf16[16,4096]{1,0:T(8,128)(2,1)S(1)} collective-permute-done((bf16[16,4096]{1,0:T(8,128)(2,1)S(1)}, bf16[16,4096]{1,0:T(8,128)(2,1)S(1)}, u32[]{:S(2)}, u32[]{:S(2)}) %collective-permute-start.17) | collective-permute-done | bytes 131104 | tf_op jit(solution)/shard_map/ppermute | solution.py:27
  56.6 0.0 collective-permute-done.14
  56.7 1.2 %collective-permute-done.19 = bf16[16,4096]{1,0:T(8,128)(2,1)S(1)} collective-permute-done((bf16[16,4096]{1,0:T(8,128)(2,1)S(1)}, bf16[16,4096]{1,0:T(8,128)(2,1)S(1)}, u32[]{:S(2)}, u32[]{:S(2)}) %collective-permute-start.19) | collective-permute-done | bytes 131104 | tf_op jit(solution)/shard_map/ppermute | solution.py:27
  57.9 0.2 collective-permute-done.20
  58.1 0.1 collective-permute-start.23
  58.2 2.1 %collective-permute-start.21 = (bf16[8,4096]{1,0:T(8,128)(2,1)S(1)}, bf16[8,4096]{1,0:T(8,128)(2,1)S(1)}, u32[]{:S(2)}, u32[]{:S(2)}) collective-permute-start(bf16[8,4096]{1,0:T(8,128)(2,1)S(1)} %get-tuple-element.53), channel_id=1, source_target_pairs={{0,3},{1,2},{2,1},{3,0},{4,7},{5,6},{6,5},{7,4},{8,11},{9,10},{10,... | collective-permute-start | bytes 196616 | tf_op jit(solution)/shard_map/ppermute | solution.py:27
  60.3 1.4 %collective-permute-start.22 = (bf16[8,4096]{1,0:T(8,128)(2,1)S(1)}, bf16[8,4096]{1,0:T(8,128)(2,1)S(1)}, u32[]{:S(2)}, u32[]{:S(2)}) collective-permute-start(bf16[8,4096]{1,0:T(8,128)(2,1)S(1)} %get-tuple-element.54), channel_id=1, source_target_pairs={{0,2},{1,3},{2,0},{3,1},{4,6},{5,7},{6,4},{7,5},{8,10},{9,11},{10,... | collective-permute-start | bytes 196616 | tf_op jit(solution)/shard_map/ppermute | solution.py:27
  61.7 1.7 %collective-permute-done.23 = bf16[8,4096]{1,0:T(8,128)(2,1)S(1)} collective-permute-done((bf16[8,4096]{1,0:T(8,128)(2,1)S(1)}, bf16[8,4096]{1,0:T(8,128)(2,1)S(1)}, u32[]{:S(2)}, u32[]{:S(2)}) %collective-permute-start.23) | collective-permute-done | bytes 65568 | tf_op jit(solution)/shard_map/ppermute | solution.py:27
  63.4 0.9 %collective-permute-done.21 = bf16[8,4096]{1,0:T(8,128)(2,1)S(1)} collective-permute-done((bf16[8,4096]{1,0:T(8,128)(2,1)S(1)}, bf16[8,4096]{1,0:T(8,128)(2,1)S(1)}, u32[]{:S(2)}, u32[]{:S(2)}) %collective-permute-start.21) | collective-permute-done | bytes 65568 | tf_op jit(solution)/shard_map/ppermute | solution.py:27
  64.3 2.1 %collective-permute-done.22 = bf16[8,4096]{1,0:T(8,128)(2,1)S(1)} collective-permute-done((bf16[8,4096]{1,0:T(8,128)(2,1)S(1)}, bf16[8,4096]{1,0:T(8,128)(2,1)S(1)}, u32[]{:S(2)}, u32[]{:S(2)}) %collective-permute-start.22) | collective-permute-done | bytes 65568 | tf_op jit(solution)/shard_map/ppermute | solution.py:27
  66.4 0.7 fusion.6
  (18 shorter events, 0.4 us)
Async XLA Ops:
  1.4 8.5 %collective-permute-start = (bf16[8,4224]{1,0:T(8,128)(2,1)S(1)}, bf16[8,4224]{1,0:T(8,128)(2,1)S(1)}, u32[]{:S(2)}, u32[]{:S(2)}) collective-permute-start(bf16[8,4224]{1,0:T(8,128)(2,1)S(1)} %shard_map.64), channel_id=1, source_target_pairs={{0,1},{1,0},{2,3},{3,2},{4,5},{5,4},{6,7},{7,6},{8,9},{9,8},{10,11... | collective-permute-start | bytes 202760 | tf_op jit(solution)/shard_map/ppermute | solution.py:27
  4.5 6.9 %collective-permute-start.2 = (bf16[8,4224]{1,0:T(8,128)(2,1)S(1)}, bf16[8,4224]{1,0:T(8,128)(2,1)S(1)}, u32[]{:S(2)}, u32[]{:S(2)}) collective-permute-start(bf16[8,4224]{1,0:T(8,128)(2,1)S(1)} %shard_map.64), channel_id=1, source_target_pairs={{0,3},{1,2},{2,1},{3,0},{4,7},{5,6},{6,5},{7,4},{8,11},{9,10},{10,... | collective-permute-start | bytes 202760 | tf_op jit(solution)/shard_map/ppermute | solution.py:27
  7.0 6.6 %collective-permute-start.1 = (bf16[8,4224]{1,0:T(8,128)(2,1)S(1)}, bf16[8,4224]{1,0:T(8,128)(2,1)S(1)}, u32[]{:S(2)}, u32[]{:S(2)}) collective-permute-start(bf16[8,4224]{1,0:T(8,128)(2,1)S(1)} %shard_map.64), channel_id=1, source_target_pairs={{0,2},{1,3},{2,0},{3,1},{4,6},{5,7},{6,4},{7,5},{8,10},{9,11},{10,... | collective-permute-start | bytes 202760 | tf_op jit(solution)/shard_map/ppermute | solution.py:27
  13.6 13.0 %collective-permute-start.4 = (bf16[16,4224]{1,0:T(8,128)(2,1)S(1)}, bf16[16,4224]{1,0:T(8,128)(2,1)S(1)}, u32[]{:S(2)}, u32[]{:S(2)}) collective-permute-start(bf16[16,4224]{1,0:T(8,128)(2,1)S(1)} %pad_maximum_fusion), channel_id=1, source_target_pairs={{0,16},{4,20},{8,24},{12,28},{16,0},{20,4},{24,8},{28,12},{1,17},{... | collective-permute-start | bytes 405512 | tf_op jit(solution)/shard_map/ppermute | solution.py:27
  15.1 6.5 %collective-permute-start.3 = (bf16[16,4224]{1,0:T(8,128)(2,1)S(1)}, bf16[16,4224]{1,0:T(8,128)(2,1)S(1)}, u32[]{:S(2)}, u32[]{:S(2)}) collective-permute-start(bf16[16,4224]{1,0:T(8,128)(2,1)S(1)} %pad_maximum_fusion), channel_id=1, source_target_pairs={{0,8},{4,12},{8,0},{12,4},{16,24},{20,28},{24,16},{28,20},{1,9},{5... | collective-permute-start | bytes 405512 | tf_op jit(solution)/shard_map/ppermute | solution.py:27
  16.6 7.9 %collective-permute-start.6 = (bf16[16,4224]{1,0:T(8,128)(2,1)S(1)}, bf16[16,4224]{1,0:T(8,128)(2,1)S(1)}, u32[]{:S(2)}, u32[]{:S(2)}) collective-permute-start(bf16[16,4224]{1,0:T(8,128)(2,1)S(1)} %pad_maximum_fusion.1), channel_id=1, source_target_pairs={{0,16},{4,20},{8,24},{12,28},{16,0},{20,4},{24,8},{28,12},{1,17},{... | collective-permute-start | bytes 405512 | tf_op jit(solution)/shard_map/ppermute | solution.py:27
  17.2 9.4 %collective-permute-start.5 = (bf16[16,4224]{1,0:T(8,128)(2,1)S(1)}, bf16[16,4224]{1,0:T(8,128)(2,1)S(1)}, u32[]{:S(2)}, u32[]{:S(2)}) collective-permute-start(bf16[16,4224]{1,0:T(8,128)(2,1)S(1)} %pad_maximum_fusion.1), channel_id=1, source_target_pairs={{0,8},{4,12},{8,0},{12,4},{16,24},{20,28},{24,16},{28,20},{1,9},{5... | collective-permute-start | bytes 405512 | tf_op jit(solution)/shard_map/ppermute | solution.py:27
  17.7 11.9 %collective-permute-start.9 = (bf16[32,4224]{1,0:T(8,128)(2,1)S(1)}, bf16[32,4224]{1,0:T(8,128)(2,1)S(1)}, u32[]{:S(2)}, u32[]{:S(2)}) collective-permute-start(bf16[32,4224]{1,0:T(8,128)(2,1)S(1)} %constant_dynamic-update-slice_fusion.refs_0_), channel_id=1, source_target_pairs={{0,4},{4,0},{8,12},{12,8},{16,20},{20,16},{24,28},{28,24},{1,5},{5... | collective-permute-start | bytes 811016 | tf_op jit(solution)/shard_map/ppermute | solution.py:27
  21.6 5.1 %collective-permute-start.7 = (bf16[16,4224]{1,0:T(8,128)(2,1)S(1)}, bf16[16,4224]{1,0:T(8,128)(2,1)S(1)}, u32[]{:S(2)}, u32[]{:S(2)}) collective-permute-start(bf16[16,4224]{1,0:T(8,128)(2,1)S(1)} %collective-permute-done.3), channel_id=1, source_target_pairs={{0,16},{4,20},{8,24},{12,28},{16,0},{20,4},{24,8},{28,12},{1,17},{... | collective-permute-start | bytes 405512 | tf_op jit(solution)/shard_map/ppermute | solution.py:27
  24.5 5.1 %collective-permute-start.8 = (bf16[16,4224]{1,0:T(8,128)(2,1)S(1)}, bf16[16,4224]{1,0:T(8,128)(2,1)S(1)}, u32[]{:S(2)}, u32[]{:S(2)}) collective-permute-start(bf16[16,4224]{1,0:T(8,128)(2,1)S(1)} %collective-permute-done.6), channel_id=1, source_target_pairs={{0,8},{4,12},{8,0},{12,4},{16,24},{20,28},{24,16},{28,20},{1,9},{5... | collective-permute-start | bytes 405512 | tf_op jit(solution)/shard_map/ppermute | solution.py:27
  26.6 4.6 %collective-permute-start.10 = (bf16[64,4224]{1,0:T(8,128)(2,1)S(1)}, bf16[64,4224]{1,0:T(8,128)(2,1)S(1)}, u32[]{:S(2)}, u32[]{:S(2)}) collective-permute-start(bf16[64,4224]{1,0:T(8,128)(2,1)S(1)} %constant_dynamic-update-slice_fusion.2.refs_1_), channel_id=1, source_target_pairs={{0,4},{4,0},{8,12},{12,8},{16,20},{20,16},{24,28},{28,24},{1,5},{5... | collective-permute-start | bytes 1622024 | tf_op jit(solution)/shard_map/ppermute | solution.py:27
  29.6 1.6 %collective-permute-start.11 = (bf16[32,4224]{1,0:T(8,128)(2,1)S(1)}, bf16[32,4224]{1,0:T(8,128)(2,1)S(1)}, u32[]{:S(2)}, u32[]{:S(2)}) collective-permute-start(bf16[32,4224]{1,0:T(8,128)(2,1)S(1)} %constant_dynamic-update-slice_fusion.6.refs_2_), channel_id=1, source_target_pairs={{0,4},{4,0},{8,12},{12,8},{16,20},{20,16},{24,28},{28,24},{1,5},{5... | collective-permute-start | bytes 811016 | tf_op jit(solution)/shard_map/ppermute | solution.py:27
  41.1 1.6 %collective-permute-start.15 = (bf16[32,4096]{1,0:T(8,128)(2,1)S(1)}, bf16[32,4096]{1,0:T(8,128)(2,1)S(1)}, u32[]{:S(2)}, u32[]{:S(2)}) collective-permute-start(bf16[32,4096]{1,0:T(8,128)(2,1)S(1)} %get-tuple-element.41), channel_id=1, source_target_pairs={{0,4},{4,0},{8,12},{12,8},{16,20},{20,16},{24,28},{28,24},{1,5},{5... | collective-permute-start | bytes 786440 | tf_op jit(solution)/shard_map/ppermute | solution.py:27
  41.3 11.0 %collective-permute-start.12 = (bf16[32,4096]{1,0:T(8,128)(2,1)S(1)}, bf16[32,4096]{1,0:T(8,128)(2,1)S(1)}, u32[]{:S(2)}, u32[]{:S(2)}) collective-permute-start(bf16[32,4096]{1,0:T(8,128)(2,1)S(1)} %get-tuple-element.37), channel_id=1, source_target_pairs={{0,4},{4,0},{8,12},{12,8},{16,20},{20,16},{24,28},{28,24},{1,5},{5... | collective-permute-start | bytes 786440 | tf_op jit(solution)/shard_map/ppermute | solution.py:27
  41.7 4.7 %collective-permute-start.13 = (bf16[64,4096]{1,0:T(8,128)(2,1)S(1)}, bf16[64,4096]{1,0:T(8,128)(2,1)S(1)}, u32[]{:S(2)}, u32[]{:S(2)}) collective-permute-start(bf16[64,4096]{1,0:T(8,128)(2,1)S(1)} %get-tuple-element.39), channel_id=1, source_target_pairs={{0,4},{4,0},{8,12},{12,8},{16,20},{20,16},{24,28},{28,24},{1,5},{5... | collective-permute-start | bytes 1572872 | tf_op jit(solution)/shard_map/ppermute | solution.py:27
  42.8 5.9 %collective-permute-start.18 = (bf16[16,4096]{1,0:T(8,128)(2,1)S(1)}, bf16[16,4096]{1,0:T(8,128)(2,1)S(1)}, u32[]{:S(2)}, u32[]{:S(2)}) collective-permute-start(bf16[16,4096]{1,0:T(8,128)(2,1)S(1)} %get-tuple-element.51), channel_id=1, source_target_pairs={{0,16},{4,20},{8,24},{12,28},{16,0},{20,4},{24,8},{28,12},{1,17},{... | collective-permute-start | bytes 393224 | tf_op jit(solution)/shard_map/ppermute | solution.py:27
  44.9 5.3 %collective-permute-start.16 = (bf16[16,4096]{1,0:T(8,128)(2,1)S(1)}, bf16[16,4096]{1,0:T(8,128)(2,1)S(1)}, u32[]{:S(2)}, u32[]{:S(2)}) collective-permute-start(bf16[16,4096]{1,0:T(8,128)(2,1)S(1)} %get-tuple-element.52), channel_id=1, source_target_pairs={{0,8},{4,12},{8,0},{12,4},{16,24},{20,28},{24,16},{28,20},{1,9},{5... | collective-permute-start | bytes 393224 | tf_op jit(solution)/shard_map/ppermute | solution.py:27
  50.2 6.4 %collective-permute-start.17 = (bf16[16,4096]{1,0:T(8,128)(2,1)S(1)}, bf16[16,4096]{1,0:T(8,128)(2,1)S(1)}, u32[]{:S(2)}, u32[]{:S(2)}) collective-permute-start(bf16[16,4096]{1,0:T(8,128)(2,1)S(1)} %get-tuple-element.48), channel_id=1, source_target_pairs={{0,16},{4,20},{8,24},{12,28},{16,0},{20,4},{24,8},{28,12},{1,17},{... | collective-permute-start | bytes 393224 | tf_op jit(solution)/shard_map/ppermute | solution.py:27
  50.6 6.0 %collective-permute-start.14 = (bf16[16,4096]{1,0:T(8,128)(2,1)S(1)}, bf16[16,4096]{1,0:T(8,128)(2,1)S(1)}, u32[]{:S(2)}, u32[]{:S(2)}) collective-permute-start(bf16[16,4096]{1,0:T(8,128)(2,1)S(1)} %get-tuple-element.50), channel_id=1, source_target_pairs={{0,8},{4,12},{8,0},{12,4},{16,24},{20,28},{24,16},{28,20},{1,9},{5... | collective-permute-start | bytes 393224 | tf_op jit(solution)/shard_map/ppermute | solution.py:27
  52.3 5.6 %collective-permute-start.19 = (bf16[16,4096]{1,0:T(8,128)(2,1)S(1)}, bf16[16,4096]{1,0:T(8,128)(2,1)S(1)}, u32[]{:S(2)}, u32[]{:S(2)}) collective-permute-start(bf16[16,4096]{1,0:T(8,128)(2,1)S(1)} %get-tuple-element.47), channel_id=1, source_target_pairs={{0,8},{4,12},{8,0},{12,4},{16,24},{20,28},{24,16},{28,20},{1,9},{5... | collective-permute-start | bytes 393224 | tf_op jit(solution)/shard_map/ppermute | solution.py:27
  52.8 5.3 %collective-permute-start.20 = (bf16[16,4096]{1,0:T(8,128)(2,1)S(1)}, bf16[16,4096]{1,0:T(8,128)(2,1)S(1)}, u32[]{:S(2)}, u32[]{:S(2)}) collective-permute-start(bf16[16,4096]{1,0:T(8,128)(2,1)S(1)} %get-tuple-element.49), channel_id=1, source_target_pairs={{0,16},{4,20},{8,24},{12,28},{16,0},{20,4},{24,8},{28,12},{1,17},{... | collective-permute-start | bytes 393224 | tf_op jit(solution)/shard_map/ppermute | solution.py:27
  58.1 5.3 %collective-permute-start.23 = (bf16[8,4096]{1,0:T(8,128)(2,1)S(1)}, bf16[8,4096]{1,0:T(8,128)(2,1)S(1)}, u32[]{:S(2)}, u32[]{:S(2)}) collective-permute-start(bf16[8,4096]{1,0:T(8,128)(2,1)S(1)} %slice.87), channel_id=1, source_target_pairs={{0,1},{1,0},{2,3},{3,2},{4,5},{5,4},{6,7},{7,6},{8,9},{9,8},{10,11... | collective-permute-start | bytes 196616 | tf_op jit(solution)/shard_map/ppermute | solution.py:27
  58.2 6.1 %collective-permute-start.21 = (bf16[8,4096]{1,0:T(8,128)(2,1)S(1)}, bf16[8,4096]{1,0:T(8,128)(2,1)S(1)}, u32[]{:S(2)}, u32[]{:S(2)}) collective-permute-start(bf16[8,4096]{1,0:T(8,128)(2,1)S(1)} %get-tuple-element.53), channel_id=1, source_target_pairs={{0,3},{1,2},{2,1},{3,0},{4,7},{5,6},{6,5},{7,4},{8,11},{9,10},{10,... | collective-permute-start | bytes 196616 | tf_op jit(solution)/shard_map/ppermute | solution.py:27
  60.3 6.1 %collective-permute-start.22 = (bf16[8,4096]{1,0:T(8,128)(2,1)S(1)}, bf16[8,4096]{1,0:T(8,128)(2,1)S(1)}, u32[]{:S(2)}, u32[]{:S(2)}) collective-permute-start(bf16[8,4096]{1,0:T(8,128)(2,1)S(1)} %get-tuple-element.54), channel_id=1, source_target_pairs={{0,2},{1,3},{2,0},{3,1},{4,6},{5,7},{6,4},{7,5},{8,10},{9,11},{10,... | collective-permute-start | bytes 196616 | tf_op jit(solution)/shard_map/ppermute | solution.py:27

commit v2 on v1

v2 whole, which is shorter than its diff:
```python
import functools

import jax
import jax.numpy as jnp
from jax import lax
from jax.experimental import pallas as pl
from jax.experimental.pallas import tpu as pltpu
from jax.sharding import PartitionSpec as P

LANES = 128
ROWS = 256
COPIES = 4
TERMS = 3
VMEM_BYTES = 36 * 1024 * 1024
IN_VMEM = pl.BlockSpec(memory_space=pltpu.VMEM)
ANYWHERE = pl.BlockSpec(memory_space=pl.ANY)


def times_rows(left, right):
    return lax.dot_general(
        left, right, (((1,), (1,)), ((), ())), preferred_element_type=jnp.float32
    )


def swap(value, axis, masks):
    count = lax.axis_size(axis)
    perm = [(i, i ^ masks[i % len(masks)]) for i in range(count)]
    return lax.ppermute(value, axis, perm)


def send(value, step):
    return swap(value.astype(jnp.bfloat16), *step)


def wide(value):
    return value.astype(jnp.float32)


CORE = ("dp", (1,))


def plane_steps():
    bits = [1 << bit for bit in range(1, lax.axis_size("dp").bit_length() - 1)]
    steps = []
    for x, y in zip(bits[: len(bits) // 2], bits[len(bits) // 2 :]):
        steps += [("dp", (x, y)), ("dp", (y, x))]
    return steps


def cat(parts):
    return parts[0] if len(parts) == 1 else jnp.concatenate(parts)


def split(value, count):
    step = value.shape[0] // count
    return [value[start : start + step] for start in range(0, value.shape[0], step)]


def gather_rows(block, load):
    depth = lax.axis_size("expert")
    column = [block] + [swap(block, "expert", (mask,)) for mask in range(1, depth)]
    *steps, last = plane_steps()
    near = cat(column[: depth // 2])
    far, held = lax.optimization_barrier((cat(column[depth // 2 :]), hold(*load)))
    near_here, far_here = swap(near, *steps[0]), swap(far, *steps[0])
    near, far = cat([near, near_here]), cat([far, far_here])
    for step in steps[1:]:
        near, far = cat([near, swap(near, *step)]), cat([far, swap(far, *step)])
    near_tail, far_tail = swap(near, *last), swap(far, *last)
    near_tail, far = lax.optimization_barrier((near_tail, far))
    near = cat([near, near_tail])
    far_tail, near_there = lax.optimization_barrier((far_tail, swap(near, *CORE)))
    far = cat([far, far_tail])
    return [near, far, near_there, swap(far, *CORE)], held


def scatter_sums(kept, away):
    near_kept, (far_kept, tail_kept) = kept[0], split(kept[1], 2)
    tail = tail_kept + wide(swap(away[2], *CORE))
    near, near_tail = split(near_kept + wide(swap(away[0], *CORE)), 2)
    far = far_kept + wide(swap(away[1], *CORE))
    *steps, last = plane_steps()
    for index, step in enumerate([last] + steps[::-1]):
        if index > 0:
            far, tail = split(far, 2)
        far_here = send(tail, step)
        if index > 0:
            far_here, near = lax.optimization_barrier((far_here, near))
            near, near_tail = split(near, 2)
        near, far = near + wide(send(near_tail, step)), far + wide(far_here)
    depth = lax.axis_size("expert")
    total, *column = split(near, depth // 2) + split(far, depth // 2)
    column = [send(part, ("expert", (mask + 1,))) for mask, part in enumerate(column)]
    near_column, far_column = column[: depth // 2 - 1], column[depth // 2 - 1 :]
    far = sum(wide(part) for part in far_column)
    far, *near_column = lax.optimization_barrier((far, *near_column))
    return sum([wide(part) for part in near_column], total + far).astype(jnp.bfloat16)


def pack_kernel(tokens_hbm, ids_hbm, router_hbm, packed_ref, tokens_ref, ids_ref, router_ref, done):
    pairs = [(tokens_hbm, tokens_ref), (ids_hbm, ids_ref), (router_hbm, router_ref)]
    copies = [
        pltpu.make_async_copy(source, target, done.at[index])
        for index, (source, target) in enumerate(pairs)
    ]
    for copy in copies:
        copy.start()
    for copy in copies:
        copy.wait()
    tokens = tokens_ref[...]
    width, expert_total = tokens.shape[1], router_ref.shape[0]
    logits = times_rows(tokens, router_ref[...])
    experts = lax.broadcasted_iota(jnp.int32, logits.shape, 1)
    ids = ids_ref[...]
    chosen = experts < 0
    for pick in range(ids.shape[1]):
        chosen = jnp.logical_or(chosen, ids[:, pick : pick + 1] == experts)
    scores = jnp.where(chosen, 1.0 / (1.0 + jnp.exp(-logits)), 0.0)
    rest = scores / jnp.sum(scores, axis=1, keepdims=True)
    place = (expert_total, packed_ref.shape[1] - width)
    source, lane = [lax.broadcasted_iota(jnp.int32, place, axis) for axis in (0, 1)]
    tags = 0.0
    for term in range(TERMS):
        part = rest.astype(jnp.bfloat16)
        rest = rest - part.astype(jnp.float32)
        moved = (lane == source + term * expert_total).astype(jnp.float32).astype(jnp.bfloat16)
        tags = tags + jnp.dot(part, moved, preferred_element_type=jnp.float32)
    packed_ref[:, :width] = tokens
    packed_ref[:, width:] = tags.astype(jnp.bfloat16)


def pack(tokens, expert_ids, router):
    rows, width = tokens.shape
    extra = -(-TERMS * router.shape[0] // LANES) * LANES
    return pl.pallas_call(
        pack_kernel,
        out_shape=pltpu.VMEM((rows, width + extra), tokens.dtype),
        in_specs=[ANYWHERE] * 3,
        out_specs=IN_VMEM,
        scratch_shapes=[
            *[pltpu.VMEM(value.shape, value.dtype) for value in (tokens, expert_ids, router)],
            pltpu.SemaphoreType.DMA((3,)),
        ],
        cost_estimate=pl.CostEstimate(
            flops=2 * rows * router.size, bytes_accessed=4 * router.size, transcendentals=0
        ),
    )(*[pltpu.with_memory_space_constraint(v, pltpu.HBM) for v in (tokens, expert_ids, router)])


def load_kernel(expert, *refs):
    *sources, held_ref, done = refs
    units = sources[0].shape[1]
    step = units // COPIES
    copies = [
        pltpu.make_async_copy(
            source.at[expert, pl.ds(part * step, step)],
            held_ref.at[pl.ds(index * units + part * step, step)],
            done.at[index * COPIES + part],
        )
        for index, source in enumerate(sources)
        for part in range(COPIES)
    ]
    for copy in copies:
        copy.start()
    for copy in copies:
        copy.wait()


def hold(expert, *weights):
    _, units, width = weights[0].shape
    return pl.pallas_call(
        functools.partial(load_kernel, expert),
        out_shape=pltpu.VMEM((len(weights) * units, width), weights[0].dtype),
        in_specs=[ANYWHERE] * len(weights),
        out_specs=IN_VMEM,
        scratch_shapes=[pltpu.SemaphoreType.DMA((len(weights) * COPIES,))],
        compiler_params=pltpu.CompilerParams(vmem_limit_bytes=1024 * 1024),
        cost_estimate=pl.CostEstimate(flops=0, bytes_accessed=0, transcendentals=0),
    )(*[pltpu.with_memory_space_constraint(weight, pltpu.HBM) for weight in weights])


def expert_kernel(exp_dev, expert_total, parts, *refs):
    pieces, refs = refs[:parts], refs[parts:]
    (held_ref, gate_hbm, up_hbm, down_hbm), refs = refs[:4], refs[4:]
    *results, rows_ref, both_ref, down_ref, done = refs
    units, width = down_ref.shape[1:]
    step = units // COPIES

    def copies(source, target, first):
        return [
            pltpu.make_async_copy(
                source.at[pl.ds(part * step, step)],
                target.at[pl.ds(part * step, step)],
                done.at[first + part],
            )
            for part in range(COPIES)
        ]

    loads, first = [[]], 0
    for local in range(1, exp_dev):
        loads.append([])
        for index, source in enumerate((gate_hbm, up_hbm)):
            target = both_ref.at[local - 1, pl.ds(index * units, units)]
            loads[local] += copies(source.at[local], target, first)
            first += COPIES
    down_loads = []
    for local in range(exp_dev):
        down_loads += copies(down_hbm.at[local], down_ref.at[local], first)
        first += COPIES
    for load in sum(loads, []) + down_loads:
        load.start()
    start = 0
    for piece in pieces:
        rows_ref[start : start + piece.shape[0]] = piece[...]
        start += piece.shape[0]
    tags = rows_ref[:, width:].astype(jnp.float32)
    lane = lax.rem(lax.broadcasted_iota(jnp.int32, tags.shape, 1), expert_total)
    first_expert = lax.axis_index("dp") * exp_dev
    hidden, shares = [], []
    for local in range(exp_dev):
        for load in loads[local]:
            load.wait()
        weights = held_ref[...] if local == 0 else both_ref[local - 1]
        both = times_rows(rows_ref[:, :width], weights)
        gate, up = both[:, :units], both[:, units:]
        hidden.append((gate / (1.0 + jnp.exp(-gate)) * up).astype(jnp.bfloat16))
        mine = jnp.where(lane == first_expert + local, tags, 0.0)
        shares.append(jnp.sum(mine, axis=1, keepdims=True))
    for load in down_loads:
        load.wait()
    block = min(512, width)

    @pl.loop(0, width // block)
    def _(index):
        columns = pl.ds(pl.multiple_of(index * block, block), block)
        total = 0.0
        for local in range(exp_dev):
            out = jnp.dot(
                hidden[local], down_ref[local, :, columns], preferred_element_type=jnp.float32
            )
            total = total + out * shares[local]
        start = 0
        for result in results:
            stop = start + result.shape[0]
            result[:, columns] = total[start:stop].astype(result.dtype)
            start = stop


def run_experts(pieces, shapes, expert_total, held, *weights):
    exp_dev, units, width = weights[0].shape
    rows = sum(piece.shape[0] for piece in pieces)
    held = pltpu.with_memory_space_constraint(held, pltpu.VMEM)
    weights = [pltpu.with_memory_space_constraint(weight, pltpu.HBM) for weight in weights]
    place = pltpu.VMEM if len(pieces) > 1 else jax.ShapeDtypeStruct
    return pl.pallas_call(
        functools.partial(expert_kernel, exp_dev, expert_total, len(pieces)),
        out_shape=[place((size, width), kind) for size, kind in shapes],
        in_specs=[IN_VMEM] * (len(pieces) + 1) + [ANYWHERE] * 3,
        out_specs=[IN_VMEM] * len(shapes),
        scratch_shapes=[
            pltpu.VMEM((rows, pieces[0].shape[1]), jnp.bfloat16),
            pltpu.VMEM((max(1, exp_dev - 1), 2 * units, width), jnp.bfloat16),
            pltpu.VMEM((exp_dev, units, width), jnp.bfloat16),
            pltpu.SemaphoreType.DMA(((3 * exp_dev - 2) * COPIES,)),
        ],
        compiler_params=pltpu.CompilerParams(vmem_limit_bytes=VMEM_BYTES),
        cost_estimate=pl.CostEstimate(
            flops=6 * rows * exp_dev * units * width,
            bytes_accessed=rows * width * 5,
            transcendentals=rows * exp_dev * units,
        ),
    )(*pieces, held, *weights)


def body(tokens, expert_ids, router, w_gate, w_up, w_down):
    pieces, held = gather_rows(pack(tokens, expert_ids, router), (0, w_gate, w_up))
    count = pieces[0].shape[0]
    shapes = [(count, jnp.float32)] * 2 + [(count, jnp.bfloat16)] + [(count // 2, jnp.bfloat16)] * 2
    operands = (router.shape[0], held, w_gate, w_up, w_down)
    if 4 * count <= ROWS:
        results = run_experts(pieces, shapes, *operands)
    else:
        rows, results, start = cat(pieces), [], 0
        for size, kind in shapes:
            chunks = [
                run_experts([rows[first : first + ROWS]], [(ROWS, kind)], *operands)[0]
                for first in range(start, start + size, ROWS)
            ]
            results.append(cat(chunks))
            start += size
    return scatter_sums(results[:2], results[2:])


def solution(mesh):
    in_specs = (
        P(("dp", "expert"), None),
        P(("dp", "expert"), None),
        P(),
        P("dp", "expert", None),
        P("dp", "expert", None),
        P("dp", "expert", None),
    )
    out_specs = P(("dp", "expert"), None)
    return jax.shard_map(body, mesh=mesh, in_specs=in_specs, out_specs=out_specs, check_vma=False)
```

time: 67.2 us -> 63 us (0.938)
  Pallas kernels: 17 us -> 15.1 us
  starting transfers between devices: 24.1 us -> 22.4 us
    pallas_call x2 -> x1, Pallas kernels: 5.72 us -> 2.86 us  [hold(): pl.pallas_call(functools.partial(load_kernel, expert), out_shape=pltpu.VM...]
    ppermute x24 -> x19, starting transfers between devices: 24.1 us -> 22.4 us  [swap(): return lax.ppermute(value, axis, perm)]
    pallas_call x1, Pallas kernels: 9.89 us -> 10.8 us  [run_experts(): pl.pallas_call(functools.partial(expert_kernel, exp_dev, expert_total, le...]
    ppermute x24 -> x19, waiting for transfers between devices: 24.5 us -> 24 us  [swap(): return lax.ppermute(value, axis, perm)]
  transfers between devices with their start and end apart: 24 -> 19, of which waited for: 14 -> 12; matrix products, arithmetic and copies ran while one was open for 1% -> 1% of each run, Pallas kernels for 9% -> 5%
where the time goes in v2:
time: 63 us; the launch traced here: 62.9 us
  waiting for transfers between devices  24 us (38%)
  starting transfers between devices  22.4 us (36%)
  Pallas kernels  15.1 us (24%)
  other arithmetic  1.06 us (2%)
    ppermute x19, waiting for transfers between devices, swap(): return lax.ppermute(value, axis, perm)  24 us
    ppermute x19, starting transfers between devices, swap(): return lax.ppermute(value, axis, perm)  22.4 us
    pallas_call x1, Pallas kernels, run_experts(): pl.pallas_call(functools.partial(expert_kernel, exp_dev, expert_total, le...  10.8 us
    pallas_call x1, Pallas kernels, hold(): pl.pallas_call(functools.partial(load_kernel, expert), out_shape=pltpu.VM...  2.86 us
    pallas_call x1, Pallas kernels, pack(): pl.pallas_call(pack_kernel, out_shape=pltpu.VMEM((rows, width + extra), t...  1.4 us
  transfers between devices with their start and end apart: 19, of which 12 were waited for; matrix products, arithmetic and copies ran while one was open for 1% of the time, Pallas kernels for 5%

profile of v2, /device:TPU:0, one launch (start us, length us, event | category | flops | bytes accessed | tf_op | source)
XLA Modules:
  0.0 62.9 jit_solution(12504565301340575315)
XLA Ops:
  0.0 1.4 %shard_map.64 = bf16[8,4224]{1,0:T(8,128)(2,1)S(1)} custom-call(bf16[8,4096]{1,0:T(8,128)(2,1)} %tokens_hbm.1, s32[8,8]{1,0:T(8,128)} %ids_hbm.1, bf16[16,4096]{1,0:T(8,128)(2,1)} %router_hbm.1), custom_call_target="tpu_custom_call" | custom-call | flops 1048576 | bytes 262144 | tf_op jit(solution)/shard_map/pallas_call | solution.py:135
  1.4 3.1 %collective-permute-start = (bf16[8,4224]{1,0:T(8,128)(2,1)S(1)}, bf16[8,4224]{1,0:T(8,128)(2,1)S(1)}, u32[]{:S(2)}, u32[]{:S(2)}) collective-permute-start(bf16[8,4224]{1,0:T(8,128)(2,1)S(1)} %shard_map.64), channel_id=1, source_target_pairs={{0,1},{1,0},{2,3},{3,2},{4,5},{5,4},{6,7},{7,6},{8,9},{9,8},{10,11... | collective-permute-start | bytes 202760 | tf_op jit(solution)/shard_map/ppermute | solution.py:28
  4.5 2.5 %collective-permute-start.4 = (bf16[8,4224]{1,0:T(8,128)(2,1)S(1)}, bf16[8,4224]{1,0:T(8,128)(2,1)S(1)}, u32[]{:S(2)}, u32[]{:S(2)}) collective-permute-start(bf16[8,4224]{1,0:T(8,128)(2,1)S(1)} %shard_map.64), channel_id=1, source_target_pairs={{0,3},{1,2},{2,1},{3,0},{4,7},{5,6},{6,5},{7,4},{8,11},{9,10},{10,... | collective-permute-start | bytes 202760 | tf_op jit(solution)/shard_map/ppermute | solution.py:28
  7.0 0.1 collective-permute-start.3
  7.1 2.9 %shard_map.65.refs_4_ = bf16[768,4096]{1,0:T(8,128)(2,1)S(1)} custom-call(bf16[2,384,4096]{2,1,0:T(8,128)(2,1)} %refs_5_.1, bf16[2,384,4096]{2,1,0:T(8,128)(2,1)} %refs_6_.1), custom_call_target="tpu_custom_call" | custom-call | tf_op jit(solution)/shard_map/pallas_call | solution.py:171
  10.0 0.0 collective-permute-done
  10.0 1.6 %collective-permute-start.1 = (bf16[16,4224]{1,0:T(8,128)(2,1)S(1)}, bf16[16,4224]{1,0:T(8,128)(2,1)S(1)}, u32[]{:S(2)}, u32[]{:S(2)}) collective-permute-start(bf16[16,4224]{1,0:T(8,128)(2,1)S(1)} %pad_maximum_fusion.2), channel_id=1, source_target_pairs={{0,8},{4,20},{8,0},{12,28},{16,24},{20,4},{24,16},{28,12},{1,9},{5... | collective-permute-start | bytes 405512 | tf_op jit(solution)/shard_map/ppermute | solution.py:28
  11.5 0.0 collective-permute-done.4
  11.5 2.0 %collective-permute-done.3 = bf16[8,4224]{1,0:T(8,128)(2,1)S(1)} collective-permute-done((bf16[8,4224]{1,0:T(8,128)(2,1)S(1)}, bf16[8,4224]{1,0:T(8,128)(2,1)S(1)}, u32[]{:S(2)}, u32[]{:S(2)}) %collective-permute-start.3) | collective-permute-done | bytes 67616 | tf_op jit(solution)/shard_map/ppermute | solution.py:28
  13.6 1.6 %collective-permute-start.5 = (bf16[16,4224]{1,0:T(8,128)(2,1)S(1)}, bf16[16,4224]{1,0:T(8,128)(2,1)S(1)}, u32[]{:S(2)}, u32[]{:S(2)}) collective-permute-start(bf16[16,4224]{1,0:T(8,128)(2,1)S(1)} %pad_maximum_fusion.3), channel_id=1, source_target_pairs={{0,8},{4,20},{8,0},{12,28},{16,24},{20,4},{24,16},{28,12},{1,9},{5... | collective-permute-start | bytes 405512 | tf_op jit(solution)/shard_map/ppermute | solution.py:28
  15.2 0.0 collective-permute-done.1
  15.2 1.6 %collective-permute-start.2 = (bf16[32,4224]{1,0:T(8,128)(2,1)S(1)}, bf16[32,4224]{1,0:T(8,128)(2,1)S(1)}, u32[]{:S(2)}, u32[]{:S(2)}) collective-permute-start(bf16[32,4224]{1,0:T(8,128)(2,1)S(1)} %pad_maximum_fusion.1), channel_id=1, source_target_pairs={{0,16},{4,12},{8,24},{12,4},{16,0},{20,28},{24,8},{28,20},{1,17},{... | collective-permute-start | bytes 811016 | tf_op jit(solution)/shard_map/ppermute | solution.py:28
  16.8 3.0 %collective-permute-done.5 = bf16[16,4224]{1,0:T(8,128)(2,1)S(1)} collective-permute-done((bf16[16,4224]{1,0:T(8,128)(2,1)S(1)}, bf16[16,4224]{1,0:T(8,128)(2,1)S(1)}, u32[]{:S(2)}, u32[]{:S(2)}) %collective-permute-start.5) | collective-permute-done | bytes 135200 | tf_op jit(solution)/shard_map/ppermute | solution.py:28
  19.8 1.9 %collective-permute-start.6 = (bf16[32,4224]{1,0:T(8,128)(2,1)S(1)}, bf16[32,4224]{1,0:T(8,128)(2,1)S(1)}, u32[]{:S(2)}, u32[]{:S(2)}) collective-permute-start(bf16[32,4224]{1,0:T(8,128)(2,1)S(1)} %constant_dynamic-update-slice_fusion), channel_id=1, source_target_pairs={{0,16},{4,12},{8,24},{12,4},{16,0},{20,28},{24,8},{28,20},{1,17},{... | collective-permute-start | bytes 811016 | tf_op jit(solution)/shard_map/ppermute | solution.py:28
  21.7 0.1 collective-permute-done.2
  21.8 0.1 collective-permute-start.7
  21.9 4.4 %collective-permute-done.6 = bf16[32,4224]{1,0:T(8,128)(2,1)S(1)} collective-permute-done((bf16[32,4224]{1,0:T(8,128)(2,1)S(1)}, bf16[32,4224]{1,0:T(8,128)(2,1)S(1)}, u32[]{:S(2)}, u32[]{:S(2)}) %collective-permute-start.6) | collective-permute-done | bytes 270368 | tf_op jit(solution)/shard_map/ppermute | solution.py:28
  26.3 0.0 collective-permute-done.7.refs_2_
  26.3 0.1 collective-permute-start.8
  26.4 1.9 %collective-permute-done.8.refs_3_ = bf16[64,4224]{1,0:T(8,128)(2,1)S(1)} collective-permute-done((bf16[64,4224]{1,0:T(8,128)(2,1)S(1)}, bf16[64,4224]{1,0:T(8,128)(2,1)S(1)}, u32[]{:S(2)}, u32[]{:S(2)}) %collective-permute-start.8) | collective-permute-done | bytes 540704 | tf_op jit(solution)/shard_map/ppermute | solution.py:28
  28.3 10.8 %shard_map.66 = (f32[64,4096]{1,0:T(8,128)S(1)}, f32[64,4096]{1,0:T(8,128)S(1)}, bf16[64,4096]{1,0:T(8,128)(2,1)S(1)}, bf16[32,4096]{1,0:T(8,128)(2,1)S(1)}, bf16[32,4096]{1,0:T(8,128)(2,1)S(1)}) custom-call(bf16[64,4224]{1,0:T(8,128)(2,1)S(1)} %pad_maximum_fusion.refs_0_, bf16[64,4224]{1,0:T(8,128)(2,1)S(1)} %constant_dynamic-update-slice_fusion.2.refs_1_, ...), custom_call_target="tpu_custom_call" | custom-call | flops 4831838208 | bytes 5242880 | tf_op jit(solution)/shard_map/pallas_call | solution.py:255
  39.2 0.2 collective-permute-start.10
  39.4 0.4 collective-permute-start.9
  39.7 0.1 collective-permute-start.13
  39.9 0.9 %collective-permute-done.10 = bf16[32,4096]{1,0:T(8,128)(2,1)S(1)} collective-permute-done((bf16[32,4096]{1,0:T(8,128)(2,1)S(1)}, bf16[32,4096]{1,0:T(8,128)(2,1)S(1)}, u32[]{:S(2)}, u32[]{:S(2)}) %collective-permute-start.10) | collective-permute-done | bytes 262176 | tf_op jit(solution)/shard_map/ppermute | solution.py:28
  40.8 1.9 %collective-permute-start.11 = (bf16[32,4096]{1,0:T(8,128)(2,1)S(1)}, bf16[32,4096]{1,0:T(8,128)(2,1)S(1)}, u32[]{:S(2)}, u32[]{:S(2)}) collective-permute-start(bf16[32,4096]{1,0:T(8,128)(2,1)S(1)} %add_convert_fusion), channel_id=1, source_target_pairs={{0,16},{4,12},{8,24},{12,4},{16,0},{20,28},{24,8},{28,20},{1,17},{... | collective-permute-start | bytes 786440 | tf_op jit(solution)/shard_map/ppermute | solution.py:28
  42.7 0.0 collective-permute-done.13
  42.7 0.1 convert_add_fusion
  42.8 1.1 %collective-permute-start.14 = (bf16[32,4096]{1,0:T(8,128)(2,1)S(1)}, bf16[32,4096]{1,0:T(8,128)(2,1)S(1)}, u32[]{:S(2)}, u32[]{:S(2)}) collective-permute-start(bf16[32,4096]{1,0:T(8,128)(2,1)S(1)} %slice.79), channel_id=1, source_target_pairs={{0,16},{4,12},{8,24},{12,4},{16,0},{20,28},{24,8},{28,20},{1,17},{... | collective-permute-start | bytes 786440 | tf_op jit(solution)/shard_map/ppermute | solution.py:28
  43.9 0.0 collective-permute-done.9
  43.9 3.3 %collective-permute-done.11 = bf16[32,4096]{1,0:T(8,128)(2,1)S(1)} collective-permute-done((bf16[32,4096]{1,0:T(8,128)(2,1)S(1)}, bf16[32,4096]{1,0:T(8,128)(2,1)S(1)}, u32[]{:S(2)}, u32[]{:S(2)}) %collective-permute-start.11) | collective-permute-done | bytes 262176 | tf_op jit(solution)/shard_map/ppermute | solution.py:28
  47.3 0.1 convert_add_fusion.1
  47.4 1.7 %collective-permute-start.12 = (bf16[16,4096]{1,0:T(8,128)(2,1)S(1)}, bf16[16,4096]{1,0:T(8,128)(2,1)S(1)}, u32[]{:S(2)}, u32[]{:S(2)}) collective-permute-start(bf16[16,4096]{1,0:T(8,128)(2,1)S(1)} %slice.81), channel_id=1, source_target_pairs={{0,8},{4,20},{8,0},{12,28},{16,24},{20,4},{24,16},{28,12},{1,9},{5... | collective-permute-start | bytes 393224 | tf_op jit(solution)/shard_map/ppermute | solution.py:28
  49.0 1.7 %collective-permute-done.14 = bf16[32,4096]{1,0:T(8,128)(2,1)S(1)} collective-permute-done((bf16[32,4096]{1,0:T(8,128)(2,1)S(1)}, bf16[32,4096]{1,0:T(8,128)(2,1)S(1)}, u32[]{:S(2)}, u32[]{:S(2)}) %collective-permute-start.14) | collective-permute-done | bytes 262176 | tf_op jit(solution)/shard_map/ppermute | solution.py:28
  50.7 1.7 %collective-permute-done.12 = bf16[16,4096]{1,0:T(8,128)(2,1)S(1)} collective-permute-done((bf16[16,4096]{1,0:T(8,128)(2,1)S(1)}, bf16[16,4096]{1,0:T(8,128)(2,1)S(1)}, u32[]{:S(2)}, u32[]{:S(2)}) %collective-permute-start.12) | collective-permute-done | bytes 131104 | tf_op jit(solution)/shard_map/ppermute | solution.py:28
  52.4 1.7 %collective-permute-start.15 = (bf16[16,4096]{1,0:T(8,128)(2,1)S(1)}, bf16[16,4096]{1,0:T(8,128)(2,1)S(1)}, u32[]{:S(2)}, u32[]{:S(2)}) collective-permute-start(bf16[16,4096]{1,0:T(8,128)(2,1)S(1)} %slice.80), channel_id=1, source_target_pairs={{0,8},{4,20},{8,0},{12,28},{16,24},{20,4},{24,16},{28,12},{1,9},{5... | collective-permute-start | bytes 393224 | tf_op jit(solution)/shard_map/ppermute | solution.py:28
  54.1 1.0 %collective-permute-start.16 = (bf16[8,4096]{1,0:T(8,128)(2,1)S(1)}, bf16[8,4096]{1,0:T(8,128)(2,1)S(1)}, u32[]{:S(2)}, u32[]{:S(2)}) collective-permute-start(bf16[8,4096]{1,0:T(8,128)(2,1)S(1)} %get-tuple-element.35), channel_id=1, source_target_pairs={{0,2},{1,3},{2,0},{3,1},{4,6},{5,7},{6,4},{7,5},{8,10},{9,11},{10,... | collective-permute-start | bytes 196616 | tf_op jit(solution)/shard_map/ppermute | solution.py:28
  55.1 1.8 %collective-permute-start.17 = (bf16[8,4096]{1,0:T(8,128)(2,1)S(1)}, bf16[8,4096]{1,0:T(8,128)(2,1)S(1)}, u32[]{:S(2)}, u32[]{:S(2)}) collective-permute-start(bf16[8,4096]{1,0:T(8,128)(2,1)S(1)} %get-tuple-element.36), channel_id=1, source_target_pairs={{0,3},{1,2},{2,1},{3,0},{4,7},{5,6},{6,5},{7,4},{8,11},{9,10},{10,... | collective-permute-start | bytes 196616 | tf_op jit(solution)/shard_map/ppermute | solution.py:28
  56.9 0.6 collective-permute-done.15
  57.5 0.3 collective-permute-start.18
  57.8 3.8 %collective-permute-done.16 = bf16[8,4096]{1,0:T(8,128)(2,1)S(1)} collective-permute-done((bf16[8,4096]{1,0:T(8,128)(2,1)S(1)}, bf16[8,4096]{1,0:T(8,128)(2,1)S(1)}, u32[]{:S(2)}, u32[]{:S(2)}) %collective-permute-start.16) | collective-permute-done | bytes 65568 | tf_op jit(solution)/shard_map/ppermute | solution.py:28
  61.6 0.0 collective-permute-done.17
  61.6 0.6 collective-permute-done.18
  62.2 0.6 %fusion.2 = bf16[8,4096]{1,0:T(8,128)(2,1)} fusion(f32[8,4096]{1,0:T(8,128)S(1)} %convert_add_fusion.3, f32[16,4096]{1,0:T(8,128)S(1)} %convert_add_fusion.2, bf16[8,4096]{1,0:T(8,128)(2,1)S(1)} %collective-permute-done.18), kind=kLoop, calls=%fused_computation.17 | loop fusion | flops 131072 | bytes 393216 | tf_op jit(solution)/shard_map/convert_element_type | solution.py:97
  (18 shorter events, 0.4 us)
Async XLA Ops:
  1.4 8.5 %collective-permute-start = (bf16[8,4224]{1,0:T(8,128)(2,1)S(1)}, bf16[8,4224]{1,0:T(8,128)(2,1)S(1)}, u32[]{:S(2)}, u32[]{:S(2)}) collective-permute-start(bf16[8,4224]{1,0:T(8,128)(2,1)S(1)} %shard_map.64), channel_id=1, source_target_pairs={{0,1},{1,0},{2,3},{3,2},{4,5},{5,4},{6,7},{7,6},{8,9},{9,8},{10,11... | collective-permute-start | bytes 202760 | tf_op jit(solution)/shard_map/ppermute | solution.py:28
  4.5 7.0 %collective-permute-start.4 = (bf16[8,4224]{1,0:T(8,128)(2,1)S(1)}, bf16[8,4224]{1,0:T(8,128)(2,1)S(1)}, u32[]{:S(2)}, u32[]{:S(2)}) collective-permute-start(bf16[8,4224]{1,0:T(8,128)(2,1)S(1)} %shard_map.64), channel_id=1, source_target_pairs={{0,3},{1,2},{2,1},{3,0},{4,7},{5,6},{6,5},{7,4},{8,11},{9,10},{10,... | collective-permute-start | bytes 202760 | tf_op jit(solution)/shard_map/ppermute | solution.py:28
  7.0 6.6 %collective-permute-start.3 = (bf16[8,4224]{1,0:T(8,128)(2,1)S(1)}, bf16[8,4224]{1,0:T(8,128)(2,1)S(1)}, u32[]{:S(2)}, u32[]{:S(2)}) collective-permute-start(bf16[8,4224]{1,0:T(8,128)(2,1)S(1)} %shard_map.64), channel_id=1, source_target_pairs={{0,2},{1,3},{2,0},{3,1},{4,6},{5,7},{6,4},{7,5},{8,10},{9,11},{10,... | collective-permute-start | bytes 202760 | tf_op jit(solution)/shard_map/ppermute | solution.py:28
  10.0 5.2 %collective-permute-start.1 = (bf16[16,4224]{1,0:T(8,128)(2,1)S(1)}, bf16[16,4224]{1,0:T(8,128)(2,1)S(1)}, u32[]{:S(2)}, u32[]{:S(2)}) collective-permute-start(bf16[16,4224]{1,0:T(8,128)(2,1)S(1)} %pad_maximum_fusion.2), channel_id=1, source_target_pairs={{0,8},{4,20},{8,0},{12,28},{16,24},{20,4},{24,16},{28,12},{1,9},{5... | collective-permute-start | bytes 405512 | tf_op jit(solution)/shard_map/ppermute | solution.py:28
  13.6 6.2 %collective-permute-start.5 = (bf16[16,4224]{1,0:T(8,128)(2,1)S(1)}, bf16[16,4224]{1,0:T(8,128)(2,1)S(1)}, u32[]{:S(2)}, u32[]{:S(2)}) collective-permute-start(bf16[16,4224]{1,0:T(8,128)(2,1)S(1)} %pad_maximum_fusion.3), channel_id=1, source_target_pairs={{0,8},{4,20},{8,0},{12,28},{16,24},{20,4},{24,16},{28,12},{1,9},{5... | collective-permute-start | bytes 405512 | tf_op jit(solution)/shard_map/ppermute | solution.py:28
  15.2 6.5 %collective-permute-start.2 = (bf16[32,4224]{1,0:T(8,128)(2,1)S(1)}, bf16[32,4224]{1,0:T(8,128)(2,1)S(1)}, u32[]{:S(2)}, u32[]{:S(2)}) collective-permute-start(bf16[32,4224]{1,0:T(8,128)(2,1)S(1)} %pad_maximum_fusion.1), channel_id=1, source_target_pairs={{0,16},{4,12},{8,24},{12,4},{16,0},{20,28},{24,8},{28,20},{1,17},{... | collective-permute-start | bytes 811016 | tf_op jit(solution)/shard_map/ppermute | solution.py:28
  19.8 6.5 %collective-permute-start.6 = (bf16[32,4224]{1,0:T(8,128)(2,1)S(1)}, bf16[32,4224]{1,0:T(8,128)(2,1)S(1)}, u32[]{:S(2)}, u32[]{:S(2)}) collective-permute-start(bf16[32,4224]{1,0:T(8,128)(2,1)S(1)} %constant_dynamic-update-slice_fusion), channel_id=1, source_target_pairs={{0,16},{4,12},{8,24},{12,4},{16,0},{20,28},{24,8},{28,20},{1,17},{... | collective-permute-start | bytes 811016 | tf_op jit(solution)/shard_map/ppermute | solution.py:28
  21.8 4.5 %collective-permute-start.7 = (bf16[64,4224]{1,0:T(8,128)(2,1)S(1)}, bf16[64,4224]{1,0:T(8,128)(2,1)S(1)}, u32[]{:S(2)}, u32[]{:S(2)}) collective-permute-start(bf16[64,4224]{1,0:T(8,128)(2,1)S(1)} %pad_maximum_fusion.refs_0_), channel_id=1, source_target_pairs={{0,4},{4,0},{8,12},{12,8},{16,20},{20,16},{24,28},{28,24},{1,5},{5... | collective-permute-start | bytes 1622024 | tf_op jit(solution)/shard_map/ppermute | solution.py:28
  26.3 2.0 %collective-permute-start.8 = (bf16[64,4224]{1,0:T(8,128)(2,1)S(1)}, bf16[64,4224]{1,0:T(8,128)(2,1)S(1)}, u32[]{:S(2)}, u32[]{:S(2)}) collective-permute-start(bf16[64,4224]{1,0:T(8,128)(2,1)S(1)} %constant_dynamic-update-slice_fusion.2.refs_1_), channel_id=1, source_target_pairs={{0,4},{4,0},{8,12},{12,8},{16,20},{20,16},{24,28},{28,24},{1,5},{5... | collective-permute-start | bytes 1622024 | tf_op jit(solution)/shard_map/ppermute | solution.py:28
  39.2 1.6 %collective-permute-start.10 = (bf16[32,4096]{1,0:T(8,128)(2,1)S(1)}, bf16[32,4096]{1,0:T(8,128)(2,1)S(1)}, u32[]{:S(2)}, u32[]{:S(2)}) collective-permute-start(bf16[32,4096]{1,0:T(8,128)(2,1)S(1)} %get-tuple-element.28), channel_id=1, source_target_pairs={{0,4},{4,0},{8,12},{12,8},{16,20},{20,16},{24,28},{28,24},{1,5},{5... | collective-permute-start | bytes 786440 | tf_op jit(solution)/shard_map/ppermute | solution.py:28
  39.4 4.5 %collective-permute-start.9 = (bf16[32,4096]{1,0:T(8,128)(2,1)S(1)}, bf16[32,4096]{1,0:T(8,128)(2,1)S(1)}, u32[]{:S(2)}, u32[]{:S(2)}) collective-permute-start(bf16[32,4096]{1,0:T(8,128)(2,1)S(1)} %get-tuple-element.27), channel_id=1, source_target_pairs={{0,4},{4,0},{8,12},{12,8},{16,20},{20,16},{24,28},{28,24},{1,5},{5... | collective-permute-start | bytes 786440 | tf_op jit(solution)/shard_map/ppermute | solution.py:28
  39.7 3.0 %collective-permute-start.13 = (bf16[64,4096]{1,0:T(8,128)(2,1)S(1)}, bf16[64,4096]{1,0:T(8,128)(2,1)S(1)}, u32[]{:S(2)}, u32[]{:S(2)}) collective-permute-start(bf16[64,4096]{1,0:T(8,128)(2,1)S(1)} %get-tuple-element.30), channel_id=1, source_target_pairs={{0,4},{4,0},{8,12},{12,8},{16,20},{20,16},{24,28},{28,24},{1,5},{5... | collective-permute-start | bytes 1572872 | tf_op jit(solution)/shard_map/ppermute | solution.py:28
  40.8 6.4 %collective-permute-start.11 = (bf16[32,4096]{1,0:T(8,128)(2,1)S(1)}, bf16[32,4096]{1,0:T(8,128)(2,1)S(1)}, u32[]{:S(2)}, u32[]{:S(2)}) collective-permute-start(bf16[32,4096]{1,0:T(8,128)(2,1)S(1)} %add_convert_fusion), channel_id=1, source_target_pairs={{0,16},{4,12},{8,24},{12,4},{16,0},{20,28},{24,8},{28,20},{1,17},{... | collective-permute-start | bytes 786440 | tf_op jit(solution)/shard_map/ppermute | solution.py:28
  42.8 7.8 %collective-permute-start.14 = (bf16[32,4096]{1,0:T(8,128)(2,1)S(1)}, bf16[32,4096]{1,0:T(8,128)(2,1)S(1)}, u32[]{:S(2)}, u32[]{:S(2)}) collective-permute-start(bf16[32,4096]{1,0:T(8,128)(2,1)S(1)} %slice.79), channel_id=1, source_target_pairs={{0,16},{4,12},{8,24},{12,4},{16,0},{20,28},{24,8},{28,20},{1,17},{... | collective-permute-start | bytes 786440 | tf_op jit(solution)/shard_map/ppermute | solution.py:28
  47.4 5.0 %collective-permute-start.12 = (bf16[16,4096]{1,0:T(8,128)(2,1)S(1)}, bf16[16,4096]{1,0:T(8,128)(2,1)S(1)}, u32[]{:S(2)}, u32[]{:S(2)}) collective-permute-start(bf16[16,4096]{1,0:T(8,128)(2,1)S(1)} %slice.81), channel_id=1, source_target_pairs={{0,8},{4,20},{8,0},{12,28},{16,24},{20,4},{24,16},{28,12},{1,9},{5... | collective-permute-start | bytes 393224 | tf_op jit(solution)/shard_map/ppermute | solution.py:28
  52.4 5.0 %collective-permute-start.15 = (bf16[16,4096]{1,0:T(8,128)(2,1)S(1)}, bf16[16,4096]{1,0:T(8,128)(2,1)S(1)}, u32[]{:S(2)}, u32[]{:S(2)}) collective-permute-start(bf16[16,4096]{1,0:T(8,128)(2,1)S(1)} %slice.80), channel_id=1, source_target_pairs={{0,8},{4,20},{8,0},{12,28},{16,24},{20,4},{24,16},{28,12},{1,9},{5... | collective-permute-start | bytes 393224 | tf_op jit(solution)/shard_map/ppermute | solution.py:28
  54.1 7.5 %collective-permute-start.16 = (bf16[8,4096]{1,0:T(8,128)(2,1)S(1)}, bf16[8,4096]{1,0:T(8,128)(2,1)S(1)}, u32[]{:S(2)}, u32[]{:S(2)}) collective-permute-start(bf16[8,4096]{1,0:T(8,128)(2,1)S(1)} %get-tuple-element.35), channel_id=1, source_target_pairs={{0,2},{1,3},{2,0},{3,1},{4,6},{5,7},{6,4},{7,5},{8,10},{9,11},{10,... | collective-permute-start | bytes 196616 | tf_op jit(solution)/shard_map/ppermute | solution.py:28
  55.1 6.5 %collective-permute-start.17 = (bf16[8,4096]{1,0:T(8,128)(2,1)S(1)}, bf16[8,4096]{1,0:T(8,128)(2,1)S(1)}, u32[]{:S(2)}, u32[]{:S(2)}) collective-permute-start(bf16[8,4096]{1,0:T(8,128)(2,1)S(1)} %get-tuple-element.36), channel_id=1, source_target_pairs={{0,3},{1,2},{2,1},{3,0},{4,7},{5,6},{6,5},{7,4},{8,11},{9,10},{10,... | collective-permute-start | bytes 196616 | tf_op jit(solution)/shard_map/ppermute | solution.py:28
  57.5 4.7 %collective-permute-start.18 = (bf16[8,4096]{1,0:T(8,128)(2,1)S(1)}, bf16[8,4096]{1,0:T(8,128)(2,1)S(1)}, u32[]{:S(2)}, u32[]{:S(2)}) collective-permute-start(bf16[8,4096]{1,0:T(8,128)(2,1)S(1)} %slice.82), channel_id=1, source_target_pairs={{0,1},{1,0},{2,3},{3,2},{4,5},{5,4},{6,7},{7,6},{8,9},{9,8},{10,11... | collective-permute-start | bytes 196616 | tf_op jit(solution)/shard_map/ppermute | solution.py:28
